TPU v7x, 256 devices: a whole 4x4x8 slice. The times are simulated.
256 devices in a mesh: seq: 64 (over y, z, core), head: 4 (over x).
Axes of the slice: x: 4, y: 4, z: 8, core: 2. Of those that a mesh axis runs over, the one named last changes fastest.
Arguments:
- queries: bfloat16 [131072, 512], P('seq', 'head'), may hold values from -6 to 6
- keys: bfloat16 [131072, 512], P('seq', 'head'), may hold values from -6 to 6
- values: bfloat16 [131072, 512], P('seq', 'head'), may hold values from -6 to 6
- delta: float32 [8, 131072], P('head', 'seq'), may hold values from -36 to 36
- dout: bfloat16 [131072, 512], P('seq', 'head'), may hold values from -48 to 48
- partner: int32 [512], P('seq'), may hold values from 0 to 511, as said below
- sort_weight: float32 [8, 64, 64], P('head'), may hold values from -0.75 to 0.75
Outputs:
- d_queries: bfloat16 [131072, 512], P('seq', 'head')
- d_keys: bfloat16 [131072, 512], P('seq', 'head')
- d_values: bfloat16 [131072, 512], P('seq', 'head')
- d_sort: float32 [8, 64, 64], P('head')
Inputs may be any that keep to these rules, and one draw needn't show every extreme that they name: partner is a permutation of the 512 blocks; the blocks of one index of seq are 8 consecutive ones, and no block's partner lies on the same index; of the blocks of one index at most 1 have partners on one other index, and every index reaches 8 others.
All inputs are finite; a program needn't handle non-finite values.
Results may differ from a plain program's by a relative error of at most 0.0095.
Values may be sent and summed in bfloat16 or wider, within the bound.
No kernel may reach another device: no remote copies, remote signals or barrier semaphores. Data moves between devices by JAX's collectives and lax.ppermute only.
A program may use at most 128 MiB of HBM per device.

v0:
```python
import math

import jax
import jax.numpy as jnp
from jax import lax
from jax.sharding import PartitionSpec as P


def partner_terms(
    queries_in,
    grads_in,
    own_max,
    own_total,
    delta_in,
    sortq_in,
    k_blocks,
    v_blocks,
    summary,
    score_scale,
):
    scores = (
        jnp.einsum("bqhd,bkhd->bhqk", queries_in, k_blocks, preferred_element_type=jnp.float32)
        * score_scale
    )
    joint_max = jnp.maximum(own_max, jnp.max(scores, axis=3))
    joint_total = own_total * jnp.exp(own_max - joint_max) + jnp.sum(
        jnp.exp(scores - joint_max[..., None]), axis=3
    )
    log_total = joint_max + jnp.log(joint_total)
    probs = jnp.exp(scores - log_total[..., None])
    probs_low = probs.astype(jnp.bfloat16)
    gates = jax.nn.sigmoid(score_scale * jnp.sum(sortq_in * summary, axis=2))
    dprobs = jnp.einsum("bqhd,bkhd->bhqk", grads_in, v_blocks, preferred_element_type=jnp.float32)
    gate_grad = jnp.sum(probs_low.astype(jnp.float32) * dprobs, axis=(2, 3))
    dscores = (probs * (gates[:, :, None, None] * dprobs - delta_in[..., None])).astype(
        jnp.bfloat16
    )
    dq_far = (
        score_scale
        * jnp.einsum("bhqk,bkhd->bqhd", dscores, k_blocks, preferred_element_type=jnp.float32)
    ).astype(jnp.bfloat16)
    dk_far = (
        score_scale
        * jnp.einsum("bhqk,bqhd->bkhd", dscores, queries_in, preferred_element_type=jnp.float32)
    ).astype(jnp.bfloat16)
    dv_far = (
        gates[:, None, :, None]
        * jnp.einsum("bhqk,bqhd->bkhd", probs_low, grads_in, preferred_element_type=jnp.float32)
    ).astype(jnp.bfloat16)
    logit_grad = gate_grad * gates * (1.0 - gates)
    sortq_grad = score_scale * logit_grad[..., None] * summary
    column_grad = score_scale * logit_grad[..., None] * sortq_in
    return (dq_far, log_total, sortq_grad, dk_far, dv_far, column_grad)


def per_device(queries, keys, values, delta, dout, partner, sort_weight):
    seq_count = lax.axis_size("seq")
    head_count = sort_weight.shape[0]
    head_width = sort_weight.shape[1]
    block_count = partner.shape[0]
    block_len = queries.shape[0] // block_count
    capacity = (block_count + seq_count - 2) // (seq_count - 1)
    slot_total = seq_count * capacity
    score_scale = 1.0 / math.sqrt(head_width)
    pool_scale = 1.0 / math.sqrt(block_len)
    block_shape = (block_count, block_len, head_count, head_width)
    q_blocks = queries.reshape(block_shape)
    k_blocks = keys.reshape(block_shape)
    v_blocks = values.reshape(block_shape)
    g_blocks = dout.reshape(block_shape)
    delta_blocks = jnp.transpose(delta.reshape(head_count, block_count, block_len), (1, 0, 2))
    summary = jnp.sum(k_blocks, axis=1, dtype=jnp.float32) * pool_scale
    sortq = jnp.einsum("bhd,hde->bhe", summary, sort_weight, precision=lax.Precision.HIGHEST)
    self_scores = (
        jnp.einsum("bqhd,bkhd->bhqk", q_blocks, k_blocks, preferred_element_type=jnp.float32)
        * score_scale
    )
    self_max = jnp.max(self_scores, axis=3)
    self_total = jnp.sum(jnp.exp(self_scores - self_max[..., None]), axis=3)
    owners = partner // block_count
    target = partner % block_count
    position = jnp.arange(block_count, dtype=jnp.int32)
    earlier = (owners[:, None] == owners[None, :]) & (position[:, None] > position[None, :])
    slot_of = owners * capacity + jnp.sum(earlier.astype(jnp.int32), axis=1)

    def pack(array):
        return jnp.zeros((slot_total,) + array.shape[1:], array.dtype).at[slot_of].set(array)

    arrived_q, arrived_g = (
        lax.all_to_all(pack(q_blocks), "seq", split_axis=0, concat_axis=0, tiled=True),
        lax.all_to_all(pack(g_blocks), "seq", split_axis=0, concat_axis=0, tiled=True),
    )
    arrived_max, arrived_total, arrived_delta, arrived_sortq, arrived_tag = (
        lax.all_to_all(pack(self_max), "seq", split_axis=0, concat_axis=0, tiled=True),
        lax.all_to_all(pack(self_total), "seq", split_axis=0, concat_axis=0, tiled=True),
        lax.all_to_all(pack(delta_blocks), "seq", split_axis=0, concat_axis=0, tiled=True),
        lax.all_to_all(pack(sortq), "seq", split_axis=0, concat_axis=0, tiled=True),
        lax.all_to_all(
            pack((target + 1).astype(jnp.float32)), "seq", split_axis=0, concat_axis=0, tiled=True
        ),
    )
    landing = arrived_tag.astype(jnp.int32) - 1
    settle_at = jnp.where(landing >= 0, landing, block_count)

    def settle(array):
        return (
            jnp.zeros((block_count,) + array.shape[1:], array.dtype)
            .at[settle_at]
            .set(array, mode="drop")
        )

    anchor = (
        jnp.zeros((block_count,), jnp.int32)
        .at[settle_at]
        .set(jnp.arange(slot_total, dtype=jnp.int32), mode="drop")
    )
    dq_far, lse_far, sortq_far, dk_far, dv_far, column_far = partner_terms(
        settle(arrived_q),
        settle(arrived_g),
        settle(arrived_max),
        settle(arrived_total),
        settle(arrived_delta),
        settle(arrived_sortq),
        k_blocks,
        v_blocks,
        summary,
        score_scale,
    )

    def unpack(array):
        return jnp.zeros((slot_total,) + array.shape[1:], array.dtype).at[anchor].set(array)

    back_dq = lax.all_to_all(unpack(dq_far), "seq", split_axis=0, concat_axis=0, tiled=True)
    back_lse, back_sortq = (
        lax.all_to_all(unpack(lse_far), "seq", split_axis=0, concat_axis=0, tiled=True),
        lax.all_to_all(unpack(sortq_far), "seq", split_axis=0, concat_axis=0, tiled=True),
    )
    dq_part = back_dq[slot_of]
    log_total = back_lse[slot_of]
    sortq_grad = back_sortq[slot_of]
    self_dprobs = jnp.einsum(
        "bqhd,bkhd->bhqk", g_blocks, v_blocks, preferred_element_type=jnp.float32
    )
    self_probs = jnp.exp(self_scores - log_total[..., None])
    self_low = self_probs.astype(jnp.bfloat16)
    self_ds = (self_probs * (self_dprobs - delta_blocks[..., None])).astype(jnp.bfloat16)
    d_queries = (
        score_scale
        * jnp.einsum("bhqk,bkhd->bqhd", self_ds, k_blocks, preferred_element_type=jnp.float32)
        + dq_part.astype(jnp.float32)
    ).astype(jnp.bfloat16)
    dk_self = score_scale * jnp.einsum(
        "bhqk,bqhd->bkhd", self_ds, q_blocks, preferred_element_type=jnp.float32
    )
    dv_self = jnp.einsum("bhqk,bqhd->bkhd", self_low, g_blocks, preferred_element_type=jnp.float32)
    row_grad = jnp.einsum("bhe,hde->bhd", sortq_grad, sort_weight, precision=lax.Precision.HIGHEST)
    d_keys = (
        dk_self + dk_far.astype(jnp.float32) + pool_scale * (row_grad + column_far)[:, None]
    ).astype(jnp.bfloat16)
    d_values = (dv_self + dv_far.astype(jnp.float32)).astype(jnp.bfloat16)
    sort_terms = jnp.einsum("bhd,bhe->hde", summary, sortq_grad, precision=lax.Precision.HIGHEST)
    d_sort = lax.psum(sort_terms, "seq")
    return (
        d_queries.reshape(queries.shape),
        d_keys.reshape(queries.shape),
        d_values.reshape(queries.shape),
        d_sort,
    )


def solution(mesh):
    in_specs = (
        P("seq", "head"),
        P("seq", "head"),
        P("seq", "head"),
        P("head", "seq"),
        P("seq", "head"),
        P("seq"),
        P("head", None, None),
    )
    out_specs = (P("seq", "head"), P("seq", "head"), P("seq", "head"), P("head", None, None))
    return jax.shard_map(
        per_device, mesh=mesh, in_specs=in_specs, out_specs=out_specs, check_vma=False
    )
```

profile of v0, /device:TPU:1, one launch (start us, length us, event | category | flops | bytes accessed | tf_op | source)
XLA Modules:
  0.0 701.4 jit_solution(8746787107632530774)
XLA Ops:
  2.9 13.2 %all-to-all-start = ((f32[64,1,1]{2,1,0:T(1,128)}), f32[64,1,1]{2,1,0:T(1,128)S(1)}, u32[]{:S(2)}, u32[]{:S(2)}) async-start(f32[64,1,1]{2,1,0:T(1,128)} %copy.215), calls=%async_computation | async-start | bytes 65536 | tf_op jit(solution)/shard_map/all_to_all | solution.py:98
  17.8 2.5 reshape.287
  22.5 2.8 all-to-all-done
  25.2 7.6 %all-to-all-start.5 = ((f32[64,1,128]{2,1,0:T(1,128)}), f32[64,1,128]{2,1,0:T(1,128)S(1)}, u32[]{:S(2)}, u32[]{:S(2)}) async-start(f32[64,1,128]{2,1,0:T(1,128)} %reshape.295), calls=%async_computation.5 | async-start | bytes 65536 | tf_op jit(solution)/shard_map/all_to_all | solution.py:97
  32.8 2.7 multiply_reduce_fusion.2
  36.2 2.0 scatter_fusion
  38.2 3.9 all-to-all-done.5
  42.0 6.5 all-to-all-start.1
  48.5 2.9 exponential_reduce_fusion.1
  52.1 2.0 scatter_fusion.4
  54.0 4.8 all-to-all-done.1
  58.9 5.5 all-to-all-start.3
  65.1 2.0 scatter_fusion.11
  67.0 7.7 %all-to-all-done.3 = f32[64,2,256]{2,1,0:T(2,128)S(1)} async-done(((f32[64,2,256]{2,1,0:T(2,128)}), f32[64,2,256]{2,1,0:T(2,128)S(1)}, u32[]{:S(2)}, u32[]{:S(2)}) %all-to-all-start.3) | async-done | bytes 131104 | tf_op jit(solution)/shard_map/all_to_all | solution.py:95
  74.7 4.9 all-to-all-start.7
  79.6 2.5 broadcast.169.clone
  82.1 2.5 scatter_fusion.2
  84.6 5.4 all-to-all-done.7
  90.0 5.4 all-to-all-start.2
  96.5 2.5 broadcast.169.clone.1
  99.0 2.5 scatter_fusion.9
  101.5 89.9 %all-to-all-done.2 = bf16[64,256,2,64]{1,3,2,0:T(8,128)(2,1)} async-done(((bf16[64,256,2,64]{1,3,2,0:T(8,128)(2,1)}), bf16[64,256,2,64]{1,3,2,0:T(8,128)(2,1)}, u32[]{:S(2)}, u32[]{:S(2)}) %all-to-all-start.2) | async-done | bytes 4194336 | tf_op jit(solution)/shard_map/all_to_all | solution.py:90
  191.4 6.0 all-to-all-start.6
  201.9 2.6 scatter_fusion.8
  204.6 2.6 scatter_fusion.1
  207.2 2.6 scatter_fusion.5
  209.8 2.6 scatter_fusion.12
  212.4 7.4 %scatter_fusion.3 = bf16[8,256,2,64]{1,3,2,0:T(8,128)(2,1)S(1)} fusion(bf16[8,256,2,64]{1,3,2,0:T(8,128)(2,1)S(1)} %broadcast.168.clone, s32[64]{0:T(128)S(1)} %fusion.49, bf16[64,256,2,64]{1,3,2,0:T(8,128)(2,1)} %all-to-all-done.2), kind=kCustom, calls=%fused_computation.8 | custom fusion | bytes 12583168 | tf_op jit(solution)/shard_map/scatter | solution.py:109
  223.4 69.9 %all-to-all-done.6 = bf16[64,256,2,64]{1,3,2,0:T(8,128)(2,1)} async-done(((bf16[64,256,2,64]{1,3,2,0:T(8,128)(2,1)}), bf16[64,256,2,64]{1,3,2,0:T(8,128)(2,1)}, u32[]{:S(2)}, u32[]{:S(2)}) %all-to-all-start.6) | async-done | bytes 4194336 | tf_op jit(solution)/shard_map/all_to_all | solution.py:91
  293.3 7.4 %scatter_fusion.10 = bf16[8,256,2,64]{1,3,2,0:T(8,128)(2,1)S(1)} fusion(bf16[8,256,2,64]{1,3,2,0:T(8,128)(2,1)S(1)} %broadcast.168.clone.1, s32[64]{0:T(128)S(1)} %fusion.49, bf16[64,256,2,64]{1,3,2,0:T(8,128)(2,1)} %all-to-all-done.6), kind=kCustom, calls=%fused_computation.15 | custom fusion | bytes 12583168 | tf_op jit(solution)/shard_map/scatter | solution.py:109
  300.7 5.2 multiply_reduce_fusion
  307.7 5.7 all-to-all-start.9
  313.5 4.6 multiply_convert_fusion
  320.7 2.0 all-to-all-done.9
  322.7 8.5 %all-to-all-start.4 = ((f32[64,2,256]{2,1,0:T(2,128)}), f32[64,2,256]{2,1,0:T(2,128)S(1)}, u32[]{:S(2)}, u32[]{:S(2)}) async-start(f32[64,2,256]{2,1,0:T(2,128)} %scatter_fusion.6), calls=%async_computation.4 | async-start | bytes 262144 | tf_op jit(solution)/shard_map/all_to_all | solution.py:135
  331.2 2.3 fusion.29
  333.5 2.5 broadcast.169
  336.0 2.7 scatter_fusion.13
  338.7 2.9 all-to-all-done.4
  341.6 7.7 %all-to-all-start.8 = ((bf16[64,256,2,64]{1,3,2,0:T(8,128)(2,1)}), bf16[64,256,2,64]{1,3,2,0:T(8,128)(2,1)}, u32[]{:S(2)}, u32[]{:S(2)}) async-start(bf16[64,256,2,64]{1,3,2,0:T(8,128)(2,1)} %scatter_fusion.13), calls=%async_computation.8 | async-start | bytes 8388608 | tf_op jit(solution)/shard_map/all_to_all | solution.py:133
  351.1 3.1 fusion.24
  356.1 320.1 %psum.7 = f32[2,64,64]{2,1,0:T(8,128)} all-reduce(f32[2,64,64]{2,1,0:T(8,128)S(1)} %fusion.39), channel_id=1, replica_groups=mesh['seq'=64,'head'=4] {'seq'}, use_global_device_ids=true, to_apply=%region_25.26 | all-reduce | flops 8192 | bytes 65536 | tf_op jit(solution)/shard_map/psum | solution.py:162
  676.8 3.1 fusion.26
  681.9 3.6 multiply_convert_fusion.1
  687.1 3.6 copy.264
  690.6 3.1 reshape.285
  693.7 2.8 gather_fusion.1
  697.7 2.4 copy.263
  (93 shorter events, 32.1 us)
Async XLA Ops:
  0.6 17.0 %copy-start = (f32[2,64,64]{2,1,0:T(8,128)S(1)}, f32[2,64,64]{2,1,0:T(8,128)}, u32[]{:S(2)}) copy-start(f32[2,64,64]{2,1,0:T(8,128)} %param.13) | copy-start | bytes 98308
  2.9 22.4 %all-to-all-start = ((f32[64,1,1]{2,1,0:T(1,128)}), f32[64,1,1]{2,1,0:T(1,128)S(1)}, u32[]{:S(2)}, u32[]{:S(2)}) async-start(f32[64,1,1]{2,1,0:T(1,128)} %copy.215), calls=%async_computation | async-start | bytes 65536 | tf_op jit(solution)/shard_map/all_to_all | solution.py:98
  17.4 202.5 %copy-start.2 = (bf16[16,8,8,256]{3,2,1,0:T(8,128)(2,1)}, bf16[16,8,8,256]{3,2,1,0:T(8,128)(2,1)S(1)}, u32[]{:S(2)}) copy-start(bf16[16,8,8,256]{3,2,1,0:T(8,128)(2,1)S(1)} %copy.275) | copy-start | bytes 1572868
  21.0 61.2 %copy-start.6 = (bf16[8,256,2,64]{1,3,2,0:T(8,128)(2,1)}, bf16[8,256,2,64]{1,3,2,0:T(8,128)(2,1)S(1)}, u32[]{:S(2)}) copy-start(bf16[8,256,2,64]{1,3,2,0:T(8,128)(2,1)S(1)} %copy.213) | copy-start | bytes 1572868
  25.2 16.8 %all-to-all-start.5 = ((f32[64,1,128]{2,1,0:T(1,128)}), f32[64,1,128]{2,1,0:T(1,128)S(1)}, u32[]{:S(2)}, u32[]{:S(2)}) async-start(f32[64,1,128]{2,1,0:T(1,128)} %reshape.295), calls=%async_computation.5 | async-start | bytes 65536 | tf_op jit(solution)/shard_map/all_to_all | solution.py:97
  32.8 32.3 %copy-start.12 = (f32[2,2048]{1,0:T(2,128)S(1)}, f32[2,2048]{1,0:T(2,128)}, u32[]{:S(2)}) copy-start(f32[2,2048]{1,0:T(2,128)} %param.10) | copy-start | bytes 49156
  42.0 16.8 %all-to-all-start.1 = ((f32[64,2,256]{2,1,0:T(2,128)}), f32[64,2,256]{2,1,0:T(2,128)S(1)}, u32[]{:S(2)}, u32[]{:S(2)}) async-start(f32[64,2,256]{2,1,0:T(2,128)} %scatter_fusion), calls=%async_computation.1 | async-start | bytes 262144 | tf_op jit(solution)/shard_map/all_to_all | solution.py:94
  58.9 15.9 %all-to-all-start.3 = ((f32[64,2,256]{2,1,0:T(2,128)}), f32[64,2,256]{2,1,0:T(2,128)S(1)}, u32[]{:S(2)}, u32[]{:S(2)}) async-start(f32[64,2,256]{2,1,0:T(2,128)} %scatter_fusion.4), calls=%async_computation.3 | async-start | bytes 262144 | tf_op jit(solution)/shard_map/all_to_all | solution.py:95
  74.7 15.2 %all-to-all-start.7 = ((f32[64,2,256]{2,1,0:T(2,128)}), f32[64,2,256]{2,1,0:T(2,128)S(1)}, u32[]{:S(2)}, u32[]{:S(2)}) async-start(f32[64,2,256]{2,1,0:T(2,128)} %scatter_fusion.11), calls=%async_computation.7 | async-start | bytes 262144 | tf_op jit(solution)/shard_map/all_to_all | solution.py:96
  84.6 10.8 %copy-start.10 = (bf16[2048,128]{1,0:T(8,128)(2,1)S(1)}, bf16[2048,128]{1,0:T(8,128)(2,1)}, u32[]{:S(2)}) copy-start(bf16[2048,128]{1,0:T(8,128)(2,1)} %param.11) | copy-start | bytes 1572868
  90.0 101.4 %all-to-all-start.2 = ((bf16[64,256,2,64]{1,3,2,0:T(8,128)(2,1)}), bf16[64,256,2,64]{1,3,2,0:T(8,128)(2,1)}, u32[]{:S(2)}, u32[]{:S(2)}) async-start(bf16[64,256,2,64]{1,3,2,0:T(8,128)(2,1)} %scatter_fusion.2), calls=%async_computation.2 | async-start | bytes 8388608 | tf_op jit(solution)/shard_map/all_to_all | solution.py:90
  96.5 94.9 %copy-start.4 = (bf16[8,256,2,64]{1,3,2,0:T(8,128)(2,1)}, bf16[8,256,2,64]{1,3,2,0:T(8,128)(2,1)S(1)}, u32[]{:S(2)}) copy-start(bf16[8,256,2,64]{1,3,2,0:T(8,128)(2,1)S(1)} %copy.220) | copy-start | bytes 1572868
  101.5 95.9 %copy-start.11 = (bf16[2048,128]{1,0:T(8,128)(2,1)S(1)}, bf16[2048,128]{1,0:T(8,128)(2,1)}, u32[]{:S(2)}) copy-start(bf16[2048,128]{1,0:T(8,128)(2,1)} %param.9) | copy-start | bytes 1572868
  191.4 101.9 %all-to-all-start.6 = ((bf16[64,256,2,64]{1,3,2,0:T(8,128)(2,1)}), bf16[64,256,2,64]{1,3,2,0:T(8,128)(2,1)}, u32[]{:S(2)}, u32[]{:S(2)}) async-start(bf16[64,256,2,64]{1,3,2,0:T(8,128)(2,1)} %scatter_fusion.9), calls=%async_computation.6 | async-start | bytes 8388608 | tf_op jit(solution)/shard_map/all_to_all | solution.py:91
  198.4 102.3 %copy-start.8 = (bf16[8,256,2,64]{1,3,2,0:T(8,128)(2,1)}, bf16[8,256,2,64]{1,3,2,0:T(8,128)(2,1)S(1)}, u32[]{:S(2)}) copy-start(bf16[8,256,2,64]{1,3,2,0:T(8,128)(2,1)S(1)} %copy.221) | copy-start | bytes 1572868
  220.7 2.0 copy-start.1
  307.7 15.0 %all-to-all-start.9 = ((f32[64,1,128]{2,1,0:T(1,128)}), f32[64,1,128]{2,1,0:T(1,128)S(1)}, u32[]{:S(2)}, u32[]{:S(2)}) async-start(f32[64,1,128]{2,1,0:T(1,128)} %reshape.297), calls=%async_computation.9 | async-start | bytes 65536 | tf_op jit(solution)/shard_map/all_to_all | solution.py:136
  322.7 18.9 %all-to-all-start.4 = ((f32[64,2,256]{2,1,0:T(2,128)}), f32[64,2,256]{2,1,0:T(2,128)S(1)}, u32[]{:S(2)}, u32[]{:S(2)}) async-start(f32[64,2,256]{2,1,0:T(2,128)} %scatter_fusion.6), calls=%async_computation.4 | async-start | bytes 262144 | tf_op jit(solution)/shard_map/all_to_all | solution.py:135
  341.6 352.1 %all-to-all-start.8 = ((bf16[64,256,2,64]{1,3,2,0:T(8,128)(2,1)}), bf16[64,256,2,64]{1,3,2,0:T(8,128)(2,1)}, u32[]{:S(2)}, u32[]{:S(2)}) async-start(bf16[64,256,2,64]{1,3,2,0:T(8,128)(2,1)} %scatter_fusion.13), calls=%async_computation.8 | async-start | bytes 8388608 | tf_op jit(solution)/shard_map/all_to_all | solution.py:133
  351.1 325.7 %copy-start.5 = (bf16[8,256,2,64]{1,3,2,0:T(8,128)(2,1)S(1)}, bf16[8,256,2,64]{1,3,2,0:T(8,128)(2,1)}, u32[]{:S(2)}) copy-start(bf16[8,256,2,64]{1,3,2,0:T(8,128)(2,1)} %copy-done.4) | copy-start | bytes 1572868
  680.6 4.9 copy-start.7
  681.9 3.6 copy-start.9
  685.5 11.0 %copy-start.3 = (bf16[16,8,8,256]{3,2,1,0:T(8,128)(2,1)S(1)}, bf16[16,8,8,256]{3,2,1,0:T(8,128)(2,1)}, u32[]{:S(2)}) copy-start(bf16[16,8,8,256]{3,2,1,0:T(8,128)(2,1)} %copy-done.2) | copy-start | bytes 1572868
where the time goes:
time: 707 us; the launch traced here: 701 us
  blocking collectives  320 us (45%)
  waiting for transfers between devices  189 us (27%)
  local copies, waits for them, and re-layouts  81.8 us (12%)
  starting transfers between devices  71 us (10%)
  matrix products  26 us (4%)
  other arithmetic  12.2 us (2%)
    psum x1, blocking collectives, per_device(): d_sort = lax.psum(sort_terms, 'seq')  320 us
    all_to_all x1, waiting for transfers between devices, per_device(): lax.all_to_all(pack(q_blocks), 'seq', split_axis=0, concat_axis=0, tiled=...  89.9 us
    all_to_all x1, waiting for transfers between devices, per_device(): lax.all_to_all(pack(g_blocks), 'seq', split_axis=0, concat_axis=0, tiled=...  69.9 us
    scatter x6, local copies, waits for them, and re-layouts, settle(): return jnp.zeros((block_count,) + array.shape[1:], array.dtype).at[settle...  25.1 us
    unnamed x38, local copies, waits for them, and re-layouts  17.3 us
  transfers between devices with their start and end apart: 10, of which 9 were waited for; matrix products, arithmetic and copies ran while one was open for 13% of the time, Pallas kernels for 0%

commit v1 on v0

v1 whole, which is shorter than its diff:
```python
import functools
import math

import jax
import jax.numpy as jnp
from jax import lax
from jax.experimental import pallas as pl
from jax.experimental.pallas import tpu as pltpu
from jax.sharding import PartitionSpec as P

F32 = jnp.float32
BF16 = jnp.bfloat16
LANES = 128
HALF = 64
SHARE_AT = 64
VMEM_LIMIT = 48 * 1024 * 1024


def dot(a, b, dims, **kw):
    return lax.dot_general(a, b, (dims, ((), ())), preferred_element_type=F32, **kw)


def head_stack(x, scale):
    lane = lax.broadcasted_iota(jnp.int32, x.shape, 1)
    x32 = x.astype(F32) * scale
    first = jnp.where(lane < HALF, x32, 0.0)
    second = jnp.where(lane < HALF, 0.0, x32)
    return jnp.concatenate([first, second], axis=0).astype(BF16)


def split3(x):
    high = x.astype(BF16).astype(F32)
    rest = x - high
    mid = rest.astype(BF16).astype(F32)
    return high, mid, (rest - mid).astype(BF16).astype(F32)


def to_rows(v):
    return jnp.concatenate([v[:, i * HALF : (i + 1) * HALF] for i in range(8)], axis=0)


def from_rows(x):
    return jnp.concatenate([x[i : i + 1, :] for i in range(8)], axis=1)


def head_rows(v):
    return jnp.concatenate([v[:, :HALF], v[:, HALF:]], axis=0)


def from_head_rows(x):
    return jnp.concatenate([x[0:1, :], x[1:2, :]], axis=1)


def block_diagonal(w_ref):
    zero = jnp.zeros((HALF, HALF), F32)
    top = jnp.concatenate([w_ref[0], zero], axis=1)
    bottom = jnp.concatenate([zero, w_ref[1]], axis=1)
    return jnp.concatenate([top, bottom], axis=0)


def head_sums(x):
    lane = lax.broadcasted_iota(jnp.int32, x.shape, 1)
    first = jnp.sum(jnp.where(lane < HALF, x, 0.0), axis=1, keepdims=True)
    second = jnp.sum(jnp.where(lane < HALF, 0.0, x), axis=1, keepdims=True)
    return jnp.where(lane < HALF, first, second)


def reorder(rows_ref, source_ref, pieces, blocks, to_blocks):
    total = pieces * blocks
    out_row = lax.broadcasted_iota(jnp.int32, (total, total), 0)
    in_row = lax.broadcasted_iota(jnp.int32, (total, total), 1)
    if to_blocks:
        wanted = (out_row & (pieces - 1)) * blocks + (out_row >> 6)
    else:
        wanted = (out_row & (blocks - 1)) * pieces + (out_row >> 3)
    pick = jnp.where(wanted == in_row, 1.0, 0.0).astype(BF16)
    width = source_ref.shape[1]
    for start in range(0, width, 256):
        stop = min(width, start + 256)
        rows_ref[:, start:stop] = dot(pick, source_ref[:, start:stop], ((1,), (0,))).astype(BF16)


def fold(block, pieces):
    return jnp.concatenate(
        [block[c * pieces : (c + 1) * pieces, :] for c in range(block.shape[0] // pieces)], axis=1
    )


def unfold(rows):
    return jnp.concatenate(
        [rows[:, c * LANES : (c + 1) * LANES] for c in range(rows.shape[1] // LANES)], axis=0
    )


def pack_kernel(partner_ref, q_ref, k_ref, g_ref, delta_ref, out_ref, summary_ref, rows_ref):
    blocks, pieces, block_len = 8, 64, 256
    score_scale = 1.0 / math.sqrt(HALF)
    pool_scale = 1.0 / math.sqrt(block_len)

    def step(j, carry):
        at = pl.ds(pl.multiple_of(j * block_len, block_len), block_len)
        qb, kb, gb = q_ref[at, :], k_ref[at, :], g_ref[at, :]
        scores = dot(kb, head_stack(qb, score_scale), ((1,), (1,)))
        top = jnp.max(scores, axis=0, keepdims=True)
        lse = top + jnp.log(jnp.sum(jnp.exp(scores - top), axis=0, keepdims=True))
        summary = jnp.sum(kb.astype(F32), axis=0, keepdims=True) * pool_scale
        summary_ref[pl.ds(j, 1), :] = summary
        delta = jnp.concatenate([delta_ref[0:1, at], delta_ref[1:2, at]], axis=1)
        stats = jnp.concatenate([to_rows(lse), to_rows(delta)], axis=0)
        parts = jnp.concatenate(split3(stats), axis=0)
        summary_parts = jnp.concatenate(
            list(split3(head_rows(summary))) + [jnp.zeros((10, HALF), F32)], axis=0
        )
        left = jnp.concatenate([parts, summary_parts], axis=0)
        lane = lax.broadcasted_iota(jnp.int32, (pieces, HALF), 1)
        place = partner_ref[j]
        right = jnp.where(
            lane == 0,
            (place // 8).astype(F32),
            jnp.where(lane == 1, (place % 8).astype(F32), 0.0),
        )
        to = pl.ds(pl.multiple_of(j * pieces, pieces), pieces)
        rows_ref[to, 0:512] = fold(qb, pieces)
        rows_ref[to, 512:1024] = fold(gb, pieces)
        rows_ref[to, 1024:1152] = jnp.concatenate([left, right], axis=1).astype(BF16)
        return carry

    lax.fori_loop(0, blocks, step, 0)
    reorder(out_ref, rows_ref, pieces, blocks, False)


def partner_pick(tags):
    rows = tags.shape[0]
    place = tags[:, HALF : HALF + 1].astype(F32) * 8.0 + tags[:, HALF + 1 : HALF + 2].astype(F32)
    lane = lax.broadcasted_iota(jnp.int32, (rows, rows), 1).astype(F32)
    return jnp.where(lane == place, 1.0, 0.0).astype(BF16)


def forward_kernel(in_ref, out_ref):
    pick = partner_pick(in_ref[:, 1024:1152])
    for start in range(0, 1152, 256):
        stop = min(1152, start + 256)
        out_ref[:, start:stop] = dot(pick, in_ref[:, start:stop], ((0,), (0,))).astype(BF16)


def backward_kernel(tags_ref, in_ref, out_ref):
    pick = partner_pick(tags_ref[...])
    for start in (0, 256):
        out_ref[:, start : start + 256] = dot(
            pick, in_ref[:, start : start + 256], ((1,), (0,))
        ).astype(BF16)
    tail = in_ref[:, 512:640]
    moved = dot(pick, tail, ((1,), (0,)))
    rows = tail.shape[0]
    total = jnp.sum(tail.astype(F32).reshape(rows // 8, 8, LANES), axis=0)
    lane8 = lax.broadcasted_iota(jnp.int32, (8, LANES), 1)
    total = total + pltpu.roll(total, LANES - 16, 1) + pltpu.roll(total, LANES - 32, 1)
    total = jnp.where((lane8 >= SHARE_AT) & (lane8 < SHARE_AT + 16), total, 0.0)
    high, mid, low = split3(total)
    share = high + pltpu.roll(mid, 16, 1) + pltpu.roll(low, 32, 1)
    share = jnp.broadcast_to(share[None], (rows // 8, 8, LANES)).reshape(rows, LANES)
    lane = lax.broadcasted_iota(jnp.int32, (rows, LANES), 1)
    out_ref[:, 512:640] = jnp.where(lane < SHARE_AT, moved, share).astype(BF16)


def far_kernel(
    in_ref,
    k_ref,
    v_ref,
    summary_ref,
    w_ref,
    out_ref,
    dk_ref,
    dv_ref,
    column_ref,
    rows_ref,
    back_ref,
    gate_ref,
    grad_ref,
):
    blocks, pieces, block_len = 8, 64, 256
    score_scale = 1.0 / math.sqrt(HALF)
    reorder(rows_ref, in_ref, pieces, blocks, True)
    arrived = []
    for j in range(blocks):
        s = rows_ref[j * pieces + 48 : j * pieces + 64, 1024:1152].astype(F32)[:, :HALF]
        arrived.append(from_head_rows(s[0:2] + s[2:4] + s[4:6]))
    summary_in = jnp.concatenate(arrived, axis=0)
    summary = summary_ref[...]
    sortq = dot(summary_in, block_diagonal(w_ref), ((1,), (0,)), precision=lax.Precision.HIGHEST)
    gates = jax.nn.sigmoid(score_scale * head_sums(sortq * summary))
    gate_ref[...] = gates

    def step(j, carry):
        at = pl.ds(pl.multiple_of(j * block_len, block_len), block_len)
        here = pl.ds(pl.multiple_of(j * pieces, pieces), pieces)
        kb, vb = k_ref[at, :], v_ref[at, :]
        qs = head_stack(unfold(rows_ref[here, 0:512]), score_scale)
        gs = head_stack(unfold(rows_ref[here, 512:1024]), 1.0)
        stats = rows_ref[here, 1024:1152].astype(F32)
        joined = stats[0:16, :HALF] + stats[16:32, :HALF] + stats[32:48, :HALF]
        own_lse = from_rows(joined[0:8])
        delta = from_rows(joined[8:16])
        gate = gate_ref[pl.ds(j, 1), :]
        gate_row = jnp.concatenate(
            [
                jnp.broadcast_to(gate[:, 0:1], (1, block_len)),
                jnp.broadcast_to(gate[:, HALF : HALF + 1], (1, block_len)),
            ],
            axis=1,
        )
        scores = dot(kb, qs, ((1,), (1,)))
        top = jnp.maximum(own_lse, jnp.max(scores, axis=0, keepdims=True))
        weights = jnp.exp(scores - top)
        total = jnp.exp(own_lse - top) + jnp.sum(weights, axis=0, keepdims=True)
        probs = weights * (1.0 / total)
        lse = top + jnp.log(total)
        low = probs.astype(BF16)
        dprobs = dot(vb, gs, ((1,), (1,)))
        gate_terms = jnp.sum(low.astype(F32) * dprobs, axis=0, keepdims=True)
        first = jnp.sum(gate_terms[:, :block_len], axis=1, keepdims=True)
        second = jnp.sum(gate_terms[:, block_len:], axis=1, keepdims=True)
        lane = lax.broadcasted_iota(jnp.int32, (1, LANES), 1)
        grad_ref[pl.ds(j, 1), :] = jnp.where(lane < HALF, first, second)
        dscores = (probs * (gate_row * dprobs - delta)).astype(BF16)
        dk_ref[at, :] = dot(dscores, qs, ((1,), (0,))).astype(BF16)
        dv_ref[at, :] = (dot(low, gs, ((1,), (0,))) * gate).astype(BF16)
        dq = dot(kb, dscores, ((0,), (0,))) * score_scale
        dq = jnp.concatenate([dq[:HALF, :block_len], dq[HALF:, block_len:]], axis=1)
        back_ref[here, 0:512] = dq.astype(BF16)
        parts = jnp.concatenate(
            list(split3(to_rows(lse))) + [jnp.zeros((pieces - 24, HALF), F32)], axis=0
        )
        back_ref[here, 512:640] = jnp.concatenate(
            [parts, jnp.zeros((pieces, HALF), F32)], axis=1
        ).astype(BF16)
        return carry

    lax.fori_loop(0, blocks, step, 0)
    logit_grad = grad_ref[...] * gates * (1.0 - gates)
    sortq_grad = score_scale * logit_grad * summary
    column_ref[...] = score_scale * logit_grad * sortq
    for j in range(blocks):
        parts = jnp.concatenate(
            list(split3(head_rows(sortq_grad[j : j + 1, :]))) + [jnp.zeros((10, HALF), F32)],
            axis=0,
        )
        back_ref[j * pieces + 32 : j * pieces + 48, 512:640] = jnp.concatenate(
            [parts, jnp.zeros((16, HALF), F32)], axis=1
        ).astype(BF16)
    reorder(out_ref, back_ref, pieces, blocks, False)
    outer = dot(summary_in, sortq_grad, ((0,), (0,)), precision=lax.Precision.HIGHEST)
    lane = lax.broadcasted_iota(jnp.int32, (LANES, LANES), 1)
    row = lax.broadcasted_iota(jnp.int32, (LANES, LANES), 0)
    outer = jnp.where(row < HALF, outer, pltpu.roll(outer, HALF, 1))
    inside = (lane >= SHARE_AT) & (lane < SHARE_AT + 16)
    for a in range(4):
        part = jnp.where(inside, pltpu.roll(outer, (SHARE_AT - 16 * a) % LANES, 1), 0.0)
        high, mid, low = split3(part)
        share = high + pltpu.roll(mid, 16, 1) + pltpu.roll(low, 32, 1)
        rows = slice(a * LANES, (a + 1) * LANES)
        out_ref[rows, 512:640] = (out_ref[rows, 512:640].astype(F32) + share).astype(BF16)


def self_kernel(
    in_ref,
    q_ref,
    k_ref,
    v_ref,
    g_ref,
    delta_ref,
    w_ref,
    dk_far_ref,
    dv_far_ref,
    column_ref,
    dq_out,
    dk_out,
    dv_out,
    sort_out,
    rows_ref,
    extra_ref,
):
    blocks, pieces, block_len = 8, 64, 256
    score_scale = 1.0 / math.sqrt(HALF)
    pool_scale = 1.0 / math.sqrt(block_len)
    reorder(rows_ref, in_ref, pieces, blocks, True)
    arrived = []
    for j in range(blocks):
        s = rows_ref[j * pieces + 32 : j * pieces + 48, 512:640].astype(F32)[:, :HALF]
        arrived.append(from_head_rows(s[0:2] + s[2:4] + s[4:6]))
    sortq_grad = jnp.concatenate(arrived, axis=0)
    row_grad = dot(
        sortq_grad, block_diagonal(w_ref), ((1,), (1,)), precision=lax.Precision.HIGHEST
    )
    extra_ref[...] = pool_scale * (row_grad + column_ref[...])

    lane = lax.broadcasted_iota(jnp.int32, (LANES, LANES), 1)
    found = jnp.zeros((LANES, LANES), F32)
    for a in range(4):
        s = in_ref[a * LANES : (a + 1) * LANES, 512:640].astype(F32)
        s = s + pltpu.roll(s, LANES - 16, 1) + pltpu.roll(s, LANES - 32, 1)
        s = pltpu.roll(s, (16 * a - SHARE_AT) % LANES, 1)
        found = found + jnp.where((lane >= 16 * a) & (lane < 16 * a + 16), s, 0.0)
    sort_out[...] = found[:, :HALF]

    def step(j, carry):
        at = pl.ds(pl.multiple_of(j * block_len, block_len), block_len)
        here = pl.ds(pl.multiple_of(j * pieces, pieces), pieces)
        kb, vb = k_ref[at, :], v_ref[at, :]
        qs = head_stack(q_ref[at, :], score_scale)
        gs = head_stack(g_ref[at, :], 1.0)
        far = rows_ref[here, 0:512].astype(F32)
        stats = rows_ref[here, 512:640].astype(F32)
        lse = from_rows(stats[0:8, :HALF] + stats[8:16, :HALF] + stats[16:24, :HALF])
        delta = jnp.concatenate([delta_ref[0:1, at], delta_ref[1:2, at]], axis=1)
        scores = dot(kb, qs, ((1,), (1,)))
        probs = jnp.exp(scores - lse)
        low = probs.astype(BF16)
        dprobs = dot(vb, gs, ((1,), (1,)))
        dscores = (probs * (dprobs - delta)).astype(BF16)
        dk = dot(dscores, qs, ((1,), (0,)))
        dk_out[at, :] = (
            dk + dk_far_ref[at, :].astype(F32) + extra_ref[pl.ds(j, 1), :]
        ).astype(BF16)
        dv = dot(low, gs, ((1,), (0,)))
        dv_out[at, :] = (dv + dv_far_ref[at, :].astype(F32)).astype(BF16)
        dq = dot(kb, dscores, ((0,), (0,))) * score_scale
        dq = jnp.concatenate(
            [
                dq[:HALF, :block_len] + far[:, :block_len],
                dq[HALF:, block_len:] + far[:, block_len:],
            ],
            axis=0,
        )
        dq_out[at, :] = dq.T.astype(BF16)
        return carry

    lax.fori_loop(0, blocks, step, 0)


def whole(memory_space=pltpu.VMEM):
    return pl.BlockSpec(memory_space=memory_space)


def call(kernel, outs, inputs, scratch=(), specs=None, flops=1 << 28):
    shapes = [jax.ShapeDtypeStruct(shape, dtype) for shape, dtype in outs]
    size = sum(math.prod(s.shape) * s.dtype.itemsize for s in shapes)
    size += sum(x.size * x.dtype.itemsize for x in inputs)
    return pl.pallas_call(
        kernel,
        out_shape=shapes,
        in_specs=specs or [whole()] * len(inputs),
        out_specs=[whole()] * len(shapes),
        scratch_shapes=list(scratch),
        compiler_params=pltpu.CompilerParams(vmem_limit_bytes=VMEM_LIMIT),
        cost_estimate=pl.CostEstimate(flops=flops, bytes_accessed=size, transcendentals=1 << 20),
    )(*inputs)


def exchange(x):
    return lax.all_to_all(x, "seq", split_axis=0, concat_axis=0, tiled=True)


def per_device(queries, keys, values, delta, dout, partner, sort_weight):
    tokens = queries.shape[0]
    rows = lax.axis_size("seq") * partner.shape[0]
    sent, summary = call(
        pack_kernel,
        [((rows, 1152), BF16), ((8, LANES), F32)],
        [partner, queries, keys, dout, delta],
        scratch=[pltpu.VMEM((rows, 1152), BF16)],
        specs=[whole(pltpu.SMEM)] + [whole()] * 4,
    )
    spread = exchange(sent)
    (moved,) = call(forward_kernel, [((rows, 1152), BF16)], [spread])
    arrived = exchange(moved)
    back, dk_far, dv_far, column = call(
        far_kernel,
        [
            ((rows, 640), BF16),
            ((tokens, LANES), BF16),
            ((tokens, LANES), BF16),
            ((8, LANES), F32),
        ],
        [arrived, keys, values, summary, sort_weight],
        scratch=[
            pltpu.VMEM((rows, 1152), BF16),
            pltpu.VMEM((rows, 640), BF16),
            pltpu.VMEM((8, LANES), F32),
            pltpu.VMEM((8, LANES), F32),
        ],
    )
    spread_back = exchange(back)
    (moved_back,) = call(
        backward_kernel, [((rows, 640), BF16)], [spread[:, 1024:1152], spread_back]
    )
    arrived_back = exchange(moved_back)
    d_queries, d_keys, d_values, d_sort = call(
        self_kernel,
        [((tokens, LANES), BF16)] * 3 + [((LANES, HALF), F32)],
        [
            arrived_back,
            queries,
            keys,
            values,
            dout,
            delta,
            sort_weight,
            dk_far,
            dv_far,
            column,
        ],
        scratch=[pltpu.VMEM((rows, 640), BF16), pltpu.VMEM((8, LANES), F32)],
    )
    return d_queries, d_keys, d_values, d_sort.reshape(sort_weight.shape)


def solution(mesh):
    in_specs = (
        P("seq", "head"),
        P("seq", "head"),
        P("seq", "head"),
        P("head", "seq"),
        P("seq", "head"),
        P("seq"),
        P("head", None, None),
    )
    out_specs = (P("seq", "head"), P("seq", "head"), P("seq", "head"), P("head", None, None))
    return jax.shard_map(
        per_device, mesh=mesh, in_specs=in_specs, out_specs=out_specs, check_vma=False
    )
```

time: 707 us -> 165 us (0.23)
  blocking collectives: 320 us -> 108 us
  waiting for transfers between devices: 189 us -> 19.5 us
  local copies, waits for them, and re-layouts: 81.8 us -> 6.89 us
  starting transfers between devices: 71 us -> 6.19 us
  matrix products: 26 us -> 0 us
  Pallas kernels: 0 us -> 23.2 us
  other arithmetic: 12.2 us -> 0 us
    psum x1 -> x0, blocking collectives: 320 us -> none  [per_device(): d_sort = lax.psum(sort_terms, 'seq')]
    all_to_all x10 -> x1, waiting for transfers between devices: 189 us -> 19.5 us  [exchange(): return lax.all_to_all(x, 'seq', split_axis=0, concat_axis=0, tiled=True)]
    all_to_all x0 -> x3, blocking collectives: none -> 108 us  [exchange(): return lax.all_to_all(x, 'seq', split_axis=0, concat_axis=0, tiled=True)]
    all_to_all x10 -> x1, starting transfers between devices: 71 us -> 6.19 us  [exchange(): return lax.all_to_all(x, 'seq', split_axis=0, concat_axis=0, tiled=True)]
    scatter x17 -> x0, local copies, waits for them, and re-layouts: 43.4 us -> none  [the longest x6 25.1 us: settle(): return jnp.zeros((block_count,) + array.shape[1:], array.dtype).at[settle...]
    dot_general x13 -> x0, matrix products: 26 us -> none  [the longest x1 5.24 us: partner_terms(): jnp.einsum('bqhd,bkhd->bhqk', grads_in, v_blocks, preferred_element_type=...]
    pallas_call x0 -> x5, Pallas kernels: none -> 23.2 us  [call(): pl.pallas_call(kernel, out_shape=shapes, in_specs=specs or [whole()] * le...]
    unnamed x38 -> x28, local copies, waits for them, and re-layouts: 17.3 us -> 6.22 us
  transfers between devices with their start and end apart: 10 -> 1, of which waited for: 9 -> 1; matrix products, arithmetic and copies ran while one was open for 13% -> 0% of each run, Pallas kernels for 0% -> 0%
where the time goes in v1:
time: 165 us; the launch traced here: 164 us
  blocking collectives  108 us (65%)
  Pallas kernels  23.2 us (14%)
  waiting for transfers between devices  19.5 us (12%)
  local copies, waits for them, and re-layouts  6.89 us (4%)
  starting transfers between devices  6.19 us (4%)
    all_to_all x3, blocking collectives, exchange(): return lax.all_to_all(x, 'seq', split_axis=0, concat_axis=0, tiled=True)  108 us
    pallas_call x5, Pallas kernels, call(): pl.pallas_call(kernel, out_shape=shapes, in_specs=specs or [whole()] * le...  23.2 us
    all_to_all x1, waiting for transfers between devices, exchange(): return lax.all_to_all(x, 'seq', split_axis=0, concat_axis=0, tiled=True)  19.5 us
    unnamed x28, local copies, waits for them, and re-layouts  6.22 us
    all_to_all x1, starting transfers between devices, exchange(): return lax.all_to_all(x, 'seq', split_axis=0, concat_axis=0, tiled=True)  6.19 us
  transfers between devices with their start and end apart: 1, of which 1 were waited for; matrix products, arithmetic and copies ran while one was open for 0% of the time, Pallas kernels for 0%

profile of v1, /device:TPU:1, one launch (start us, length us, event | category | flops | bytes accessed | tf_op | source)
XLA Modules:
  0.0 164.5 jit_solution(14272664495647827215)
XLA Ops:
  0.6 0.0 copy-start
  0.6 1.0 copy-done
  1.7 0.0 copy-start.3
  1.7 1.0 copy-done.3
  2.7 0.0 copy-start.5
  2.7 1.0 copy-done.5
  3.8 0.0 copy-start.11
  3.8 0.7 copy-done.11
  4.5 0.0 copy-start.13
  4.5 0.7 copy-done.13
  5.1 4.8 %shard_map.102 = (bf16[512,1152]{1,0:T(8,128)(2,1)S(1)}, f32[8,128]{1,0:T(8,128)S(1)}) custom-call(s32[8]{0:T(128)S(1)} %copy-done.13, bf16[2048,128]{1,0:T(8,128)(2,1)S(1)} %copy-done.3, bf16[2048,128]{1,0:T(8,128)(2,1)S(1)} %copy-done, bf16[2048,128]{1,0:T(8,128)(2,1)S(1)} %copy-done.5, f32[2,2048]{1,0:T(2,128)S(1)} %copy-done.11), custom_call_target="tpu_custom_call" | custom-call | flops 268435456 | bytes 2773024 | tf_op jit(solution)/shard_map/pallas_call | solution.py:349
  10.0 44.3 %all_to_all.44 = bf16[64,8,1152]{2,1,0:T(8,128)(2,1)S(1)} all-to-all(bf16[64,8,1152]{2,1,0:T(8,128)(2,1)S(1)} %bitcast.14), channel_id=1, replica_groups=mesh['seq'=64,'head'=4] {'seq'}, dimensions={0} | all-to-all | bytes 2359296 | tf_op jit(solution)/shard_map/all_to_all | solution.py:361
  54.3 1.1 shard_map.103
  55.4 0.0 copy-start.1
  55.4 0.0 copy-start.2
  55.4 0.0 copy-start.9
  55.4 37.5 %all_to_all.45 = bf16[64,8,1152]{2,1,0:T(8,128)(2,1)S(1)} all-to-all(bf16[64,8,1152]{2,1,0:T(8,128)(2,1)S(1)} %bitcast.12), channel_id=1, replica_groups=mesh['seq'=64,'head'=4] {'seq'}, dimensions={0} | all-to-all | bytes 2359296 | tf_op jit(solution)/shard_map/all_to_all | solution.py:361
  92.9 0.0 copy-done.1
  92.9 0.0 copy-done.2
  92.9 0.0 copy-done.9
  92.9 9.5 %shard_map.104 = (bf16[512,640]{1,0:T(8,128)(2,1)}, bf16[2048,128]{1,0:T(8,128)(2,1)S(1)}, bf16[2048,128]{1,0:T(8,128)(2,1)S(1)}, f32[8,128]{1,0:T(8,128)S(1)}) custom-call(bf16[512,1152]{1,0:T(8,128)(2,1)S(1)} %bitcast.11, bf16[2048,128]{1,0:T(8,128)(2,1)S(1)} %copy-done.1, bf16[2048,128]{1,0:T(8,128)(2,1)S(1)} %copy-done.2, ...), custom_call_target="tpu_custom_call" | custom-call | flops 268435456 | bytes 3973120 | tf_op jit(solution)/shard_map/pallas_call | solution.py:349
  102.4 0.0 copy-start.7
  102.4 0.8 copy-done.7
  103.2 6.2 %all-to-all-start.2 = ((bf16[64,8,640]{2,1,0:T(8,128)(2,1)}), bf16[64,8,640]{2,1,0:T(8,128)(2,1)S(1)}, u32[]{:S(2)}, u32[]{:S(2)}) async-start(bf16[64,8,640]{2,1,0:T(8,128)(2,1)} %bitcast.4), calls=%async_computation.2 | async-start | bytes 1310720 | tf_op jit(solution)/shard_map/all_to_all | solution.py:361
  109.4 0.7 slice.4.tags_ref
  110.0 19.5 %all-to-all-done.2 = bf16[64,8,640]{2,1,0:T(8,128)(2,1)S(1)} async-done(((bf16[64,8,640]{2,1,0:T(8,128)(2,1)}), bf16[64,8,640]{2,1,0:T(8,128)(2,1)S(1)}, u32[]{:S(2)}, u32[]{:S(2)}) %all-to-all-start.2) | async-done | bytes 655392 | tf_op jit(solution)/shard_map/all_to_all | solution.py:361
  129.5 0.0 copy-start.10
  129.5 0.9 copy-done.10
  130.4 0.0 copy-start.4
  130.4 0.0 copy-start.6
  130.4 0.0 copy-start.8
  130.4 0.0 copy-start.12
  130.4 0.8 shard_map.105
  131.2 26.2 %all_to_all.46 = bf16[64,8,640]{2,1,0:T(8,128)(2,1)S(1)} all-to-all(bf16[64,8,640]{2,1,0:T(8,128)(2,1)S(1)} %bitcast.16), channel_id=1, replica_groups=mesh['seq'=64,'head'=4] {'seq'}, dimensions={0} | all-to-all | bytes 1310720 | tf_op jit(solution)/shard_map/all_to_all | solution.py:361
  157.4 0.0 copy-done.4
  157.4 0.0 copy-done.6
  157.4 0.0 copy-done.8
  157.5 0.0 copy-done.12
  157.5 7.0 %shard_map.106 = (bf16[2048,128]{1,0:T(8,128)(2,1)}, bf16[2048,128]{1,0:T(8,128)(2,1)}, bf16[2048,128]{1,0:T(8,128)(2,1)}, f32[128,64]{1,0:T(8,128)}) custom-call(bf16[512,640]{1,0:T(8,128)(2,1)S(1)} %bitcast.13, bf16[2048,128]{1,0:T(8,128)(2,1)S(1)} %copy-done.4, bf16[2048,128]{1,0:T(8,128)(2,1)S(1)} %copy-done.1, bf16[2048,128]{1,0:T(8,128)(2,1)S(1)} %copy-done.2, ...), custom_call_target="tpu_custom_call" | custom-call | flops 268435456 | bytes 5459968 | tf_op jit(solution)/shard_map/pallas_call | solution.py:349
Async XLA Ops:
  0.6 1.0 copy-start
  1.7 1.0 copy-start.3
  2.7 1.0 copy-start.5
  3.8 0.7 copy-start.11
  4.5 0.7 copy-start.13
  55.4 37.5 %copy-start.1 = (bf16[2048,128]{1,0:T(8,128)(2,1)S(1)}, bf16[2048,128]{1,0:T(8,128)(2,1)}, u32[]{:S(2)}) copy-start(bf16[2048,128]{1,0:T(8,128)(2,1)} %k_ref.5) | copy-start | bytes 1572868
  55.4 37.5 %copy-start.2 = (bf16[2048,128]{1,0:T(8,128)(2,1)S(1)}, bf16[2048,128]{1,0:T(8,128)(2,1)}, u32[]{:S(2)}) copy-start(bf16[2048,128]{1,0:T(8,128)(2,1)} %v_ref.3) | copy-start | bytes 1572868
  55.4 37.5 %copy-start.9 = (f32[2,64,64]{2,1,0:T(8,128)S(1)}, f32[2,64,64]{2,1,0:T(8,128)}, u32[]{:S(2)}) copy-start(f32[2,64,64]{2,1,0:T(8,128)} %w_ref.3) | copy-start | bytes 98308
  102.4 0.8 copy-start.7
  103.2 26.3 %all-to-all-start.2 = ((bf16[64,8,640]{2,1,0:T(8,128)(2,1)}), bf16[64,8,640]{2,1,0:T(8,128)(2,1)S(1)}, u32[]{:S(2)}, u32[]{:S(2)}) async-start(bf16[64,8,640]{2,1,0:T(8,128)(2,1)} %bitcast.4), calls=%async_computation.2 | async-start | bytes 1310720 | tf_op jit(solution)/shard_map/all_to_all | solution.py:361
  129.5 0.9 copy-start.10
  130.4 27.0 %copy-start.4 = (bf16[2048,128]{1,0:T(8,128)(2,1)S(1)}, bf16[2048,128]{1,0:T(8,128)(2,1)}, u32[]{:S(2)}) copy-start(bf16[2048,128]{1,0:T(8,128)(2,1)} %q_ref.3) | copy-start | bytes 1572868
  130.4 27.0 %copy-start.6 = (bf16[2048,128]{1,0:T(8,128)(2,1)S(1)}, bf16[2048,128]{1,0:T(8,128)(2,1)}, u32[]{:S(2)}) copy-start(bf16[2048,128]{1,0:T(8,128)(2,1)} %g_ref.3) | copy-start | bytes 1572868
  130.4 27.0 %copy-start.8 = (bf16[2048,128]{1,0:T(8,128)(2,1)S(1)}, bf16[2048,128]{1,0:T(8,128)(2,1)}, u32[]{:S(2)}) copy-start(bf16[2048,128]{1,0:T(8,128)(2,1)} %copy-done.7) | copy-start | bytes 1572868
  130.4 27.0 %copy-start.12 = (f32[2,2048]{1,0:T(2,128)S(1)}, f32[2,2048]{1,0:T(2,128)}, u32[]{:S(2)}) copy-start(f32[2,2048]{1,0:T(2,128)} %delta_ref.3) | copy-start | bytes 49156

commit v2 on v1

--- a/solution.py
+++ b/solution.py
@@ -116,8 +116,8 @@
         place = partner_ref[j]
         right = jnp.where(
             lane == 0,
-            (place // 8).astype(F32),
-            jnp.where(lane == 1, (place % 8).astype(F32), 0.0),
+            (place >> 3).astype(F32),
+            jnp.where(lane == 1, (place & 7).astype(F32), 0.0),
         )
         to = pl.ds(pl.multiple_of(j * pieces, pieces), pieces)
         rows_ref[to, 0:512] = fold(qb, pieces)
@@ -125,7 +125,7 @@
         rows_ref[to, 1024:1152] = jnp.concatenate([left, right], axis=1).astype(BF16)
         return carry
 
-    lax.fori_loop(0, blocks, step, 0)
+    lax.fori_loop(0, blocks, step, 0, unroll=True)
     reorder(out_ref, rows_ref, pieces, blocks, False)
 
 
@@ -236,7 +236,7 @@
         ).astype(BF16)
         return carry
 
-    lax.fori_loop(0, blocks, step, 0)
+    lax.fori_loop(0, blocks, step, 0, unroll=True)
     logit_grad = grad_ref[...] * gates * (1.0 - gates)
     sortq_grad = score_scale * logit_grad * summary
     column_ref[...] = score_scale * logit_grad * sortq
@@ -335,7 +335,7 @@
         dq_out[at, :] = dq.T.astype(BF16)
         return carry
 
-    lax.fori_loop(0, blocks, step, 0)
+    lax.fori_loop(0, blocks, step, 0, unroll=True)
 
 
 def whole(memory_space=pltpu.VMEM):

time: 165 us -> 159 us (0.964)
  Pallas kernels: 23.2 us -> 17.3 us
    pallas_call x5, Pallas kernels: 23.2 us -> 17.3 us  [call(): pl.pallas_call(kernel, out_shape=shapes, in_specs=specs or [whole()] * le...]
where the time goes in v2:
time: 159 us
  blocking collectives  108 us (68%)
  waiting for transfers between devices  19.5 us (12%)
  Pallas kernels  17.3 us (11%)
  local copies, waits for them, and re-layouts  6.89 us (4%)
  starting transfers between devices  6.19 us (4%)
    all_to_all x3, blocking collectives, exchange(): return lax.all_to_all(x, 'seq', split_axis=0, concat_axis=0, tiled=True)  108 us
    all_to_all x1, waiting for transfers between devices, exchange(): return lax.all_to_all(x, 'seq', split_axis=0, concat_axis=0, tiled=True)  19.5 us
    pallas_call x5, Pallas kernels, call(): pl.pallas_call(kernel, out_shape=shapes, in_specs=specs or [whole()] * le...  17.3 us
    unnamed x28, local copies, waits for them, and re-layouts  6.22 us
    all_to_all x1, starting transfers between devices, exchange(): return lax.all_to_all(x, 'seq', split_axis=0, concat_axis=0, tiled=True)  6.19 us
  transfers between devices with their start and end apart: 1, of which 1 were waited for; matrix products, arithmetic and copies ran while one was open for 0% of the time, Pallas kernels for 0%

profile of v2, /device:TPU:1, one launch (start us, length us, event | category | flops | bytes accessed | tf_op | source)
XLA Modules:
  0.0 158.6 jit_solution(16053133691311048452)
XLA Ops:
  0.6 0.0 copy-start
  0.6 1.0 copy-done
  1.7 0.0 copy-start.3
  1.7 1.0 copy-done.3
  2.7 0.0 copy-start.5
  2.7 1.0 copy-done.5
  3.8 0.0 copy-start.11
  3.8 0.7 copy-done.11
  4.5 0.0 copy-start.13
  4.5 0.7 copy-done.13
  5.1 2.9 %shard_map.102 = (bf16[512,1152]{1,0:T(8,128)(2,1)S(1)}, f32[8,128]{1,0:T(8,128)S(1)}) custom-call(s32[8]{0:T(128)S(1)} %copy-done.13, bf16[2048,128]{1,0:T(8,128)(2,1)S(1)} %copy-done.3, bf16[2048,128]{1,0:T(8,128)(2,1)S(1)} %copy-done, bf16[2048,128]{1,0:T(8,128)(2,1)S(1)} %copy-done.5, f32[2,2048]{1,0:T(2,128)S(1)} %copy-done.11), custom_call_target="tpu_custom_call" | custom-call | flops 268435456 | bytes 2773024 | tf_op jit(solution)/shard_map/pallas_call | solution.py:349
  8.0 44.3 %all_to_all.44 = bf16[64,8,1152]{2,1,0:T(8,128)(2,1)S(1)} all-to-all(bf16[64,8,1152]{2,1,0:T(8,128)(2,1)S(1)} %bitcast.14), channel_id=1, replica_groups=mesh['seq'=64,'head'=4] {'seq'}, dimensions={0} | all-to-all | bytes 2359296 | tf_op jit(solution)/shard_map/all_to_all | solution.py:361
  52.4 1.1 shard_map.103
  53.4 0.0 copy-start.1
  53.4 0.0 copy-start.2
  53.4 0.0 copy-start.9
  53.5 37.5 %all_to_all.45 = bf16[64,8,1152]{2,1,0:T(8,128)(2,1)S(1)} all-to-all(bf16[64,8,1152]{2,1,0:T(8,128)(2,1)S(1)} %bitcast.12), channel_id=1, replica_groups=mesh['seq'=64,'head'=4] {'seq'}, dimensions={0} | all-to-all | bytes 2359296 | tf_op jit(solution)/shard_map/all_to_all | solution.py:361
  90.9 0.0 copy-done.1
  90.9 0.0 copy-done.2
  90.9 0.0 copy-done.9
  91.0 7.4 %shard_map.104 = (bf16[512,640]{1,0:T(8,128)(2,1)}, bf16[2048,128]{1,0:T(8,128)(2,1)S(1)}, bf16[2048,128]{1,0:T(8,128)(2,1)S(1)}, f32[8,128]{1,0:T(8,128)S(1)}) custom-call(bf16[512,1152]{1,0:T(8,128)(2,1)S(1)} %bitcast.11, bf16[2048,128]{1,0:T(8,128)(2,1)S(1)} %copy-done.1, bf16[2048,128]{1,0:T(8,128)(2,1)S(1)} %copy-done.2, ...), custom_call_target="tpu_custom_call" | custom-call | flops 268435456 | bytes 3973120 | tf_op jit(solution)/shard_map/pallas_call | solution.py:349
  98.3 0.0 copy-start.7
  98.3 0.8 copy-done.7
  99.1 6.2 %all-to-all-start.2 = ((bf16[64,8,640]{2,1,0:T(8,128)(2,1)}), bf16[64,8,640]{2,1,0:T(8,128)(2,1)S(1)}, u32[]{:S(2)}, u32[]{:S(2)}) async-start(bf16[64,8,640]{2,1,0:T(8,128)(2,1)} %bitcast.4), calls=%async_computation.2 | async-start | bytes 1310720 | tf_op jit(solution)/shard_map/all_to_all | solution.py:361
  105.3 0.7 slice.4.tags_ref
  106.0 19.5 %all-to-all-done.2 = bf16[64,8,640]{2,1,0:T(8,128)(2,1)S(1)} async-done(((bf16[64,8,640]{2,1,0:T(8,128)(2,1)}), bf16[64,8,640]{2,1,0:T(8,128)(2,1)S(1)}, u32[]{:S(2)}, u32[]{:S(2)}) %all-to-all-start.2) | async-done | bytes 655392 | tf_op jit(solution)/shard_map/all_to_all | solution.py:361
  125.5 0.0 copy-start.10
  125.5 0.9 copy-done.10
  126.4 0.0 copy-start.4
  126.4 0.0 copy-start.6
  126.4 0.0 copy-start.8
  126.4 0.0 copy-start.12
  126.4 0.8 shard_map.105
  127.2 26.2 %all_to_all.46 = bf16[64,8,640]{2,1,0:T(8,128)(2,1)S(1)} all-to-all(bf16[64,8,640]{2,1,0:T(8,128)(2,1)S(1)} %bitcast.16), channel_id=1, replica_groups=mesh['seq'=64,'head'=4] {'seq'}, dimensions={0} | all-to-all | bytes 1310720 | tf_op jit(solution)/shard_map/all_to_all | solution.py:361
  153.4 0.0 copy-done.4
  153.4 0.0 copy-done.6
  153.4 0.0 copy-done.8
  153.4 0.0 copy-done.12
  153.4 5.2 %shard_map.106 = (bf16[2048,128]{1,0:T(8,128)(2,1)}, bf16[2048,128]{1,0:T(8,128)(2,1)}, bf16[2048,128]{1,0:T(8,128)(2,1)}, f32[128,64]{1,0:T(8,128)}) custom-call(bf16[512,640]{1,0:T(8,128)(2,1)S(1)} %bitcast.13, bf16[2048,128]{1,0:T(8,128)(2,1)S(1)} %copy-done.4, bf16[2048,128]{1,0:T(8,128)(2,1)S(1)} %copy-done.1, bf16[2048,128]{1,0:T(8,128)(2,1)S(1)} %copy-done.2, ...), custom_call_target="tpu_custom_call" | custom-call | flops 268435456 | bytes 5459968 | tf_op jit(solution)/shard_map/pallas_call | solution.py:349
Async XLA Ops:
  0.6 1.0 copy-start
  1.7 1.0 copy-start.3
  2.7 1.0 copy-start.5
  3.8 0.7 copy-start.11
  4.5 0.7 copy-start.13
  53.4 37.5 %copy-start.1 = (bf16[2048,128]{1,0:T(8,128)(2,1)S(1)}, bf16[2048,128]{1,0:T(8,128)(2,1)}, u32[]{:S(2)}) copy-start(bf16[2048,128]{1,0:T(8,128)(2,1)} %k_ref.5) | copy-start | bytes 1572868
  53.4 37.5 %copy-start.2 = (bf16[2048,128]{1,0:T(8,128)(2,1)S(1)}, bf16[2048,128]{1,0:T(8,128)(2,1)}, u32[]{:S(2)}) copy-start(bf16[2048,128]{1,0:T(8,128)(2,1)} %v_ref.3) | copy-start | bytes 1572868
  53.4 37.5 %copy-start.9 = (f32[2,64,64]{2,1,0:T(8,128)S(1)}, f32[2,64,64]{2,1,0:T(8,128)}, u32[]{:S(2)}) copy-start(f32[2,64,64]{2,1,0:T(8,128)} %w_ref.3) | copy-start | bytes 98308
  98.3 0.8 copy-start.7
  99.1 26.3 %all-to-all-start.2 = ((bf16[64,8,640]{2,1,0:T(8,128)(2,1)}), bf16[64,8,640]{2,1,0:T(8,128)(2,1)S(1)}, u32[]{:S(2)}, u32[]{:S(2)}) async-start(bf16[64,8,640]{2,1,0:T(8,128)(2,1)} %bitcast.4), calls=%async_computation.2 | async-start | bytes 1310720 | tf_op jit(solution)/shard_map/all_to_all | solution.py:361
  125.5 0.9 copy-start.10
  126.4 27.0 %copy-start.4 = (bf16[2048,128]{1,0:T(8,128)(2,1)S(1)}, bf16[2048,128]{1,0:T(8,128)(2,1)}, u32[]{:S(2)}) copy-start(bf16[2048,128]{1,0:T(8,128)(2,1)} %q_ref.3) | copy-start | bytes 1572868
  126.4 27.0 %copy-start.6 = (bf16[2048,128]{1,0:T(8,128)(2,1)S(1)}, bf16[2048,128]{1,0:T(8,128)(2,1)}, u32[]{:S(2)}) copy-start(bf16[2048,128]{1,0:T(8,128)(2,1)} %g_ref.3) | copy-start | bytes 1572868
  126.4 27.0 %copy-start.8 = (bf16[2048,128]{1,0:T(8,128)(2,1)S(1)}, bf16[2048,128]{1,0:T(8,128)(2,1)}, u32[]{:S(2)}) copy-start(bf16[2048,128]{1,0:T(8,128)(2,1)} %copy-done.7) | copy-start | bytes 1572868
  126.4 27.0 %copy-start.12 = (f32[2,2048]{1,0:T(2,128)S(1)}, f32[2,2048]{1,0:T(2,128)}, u32[]{:S(2)}) copy-start(f32[2,2048]{1,0:T(2,128)} %delta_ref.3) | copy-start | bytes 49156

commit v3 on v2

--- a/solution.py
+++ b/solution.py
@@ -14,6 +14,7 @@
 HALF = 64
 SHARE_AT = 64
 VMEM_LIMIT = 48 * 1024 * 1024
+WHOLE_LIMIT = 62240000
 
 
 def dot(a, b, dims, **kw):
@@ -65,19 +66,43 @@
     return jnp.where(lane < HALF, first, second)
 
 
-def reorder(rows_ref, source_ref, pieces, blocks, to_blocks):
-    total = pieces * blocks
+def pick_rows(total, inner):
     out_row = lax.broadcasted_iota(jnp.int32, (total, total), 0)
     in_row = lax.broadcasted_iota(jnp.int32, (total, total), 1)
-    if to_blocks:
-        wanted = (out_row & (pieces - 1)) * blocks + (out_row >> 6)
-    else:
-        wanted = (out_row & (blocks - 1)) * pieces + (out_row >> 3)
-    pick = jnp.where(wanted == in_row, 1.0, 0.0).astype(BF16)
-    width = source_ref.shape[1]
-    for start in range(0, width, 256):
-        stop = min(width, start + 256)
-        rows_ref[:, start:stop] = dot(pick, source_ref[:, start:stop], ((1,), (0,))).astype(BF16)
+    outer = total // inner
+    wanted = (out_row & (outer - 1)) * inner + (out_row >> int(math.log2(outer)))
+    return jnp.where(wanted == in_row, 1.0, 0.0).astype(BF16)
+
+
+def chunks(width):
+    return [(start, min(width, start + 256)) for start in range(0, width, 256)]
+
+
+def to_blocks(rows_ref, source_ref, pieces, blocks):
+    half = pieces // 2
+    total = half * blocks
+    pick = pick_rows(total, blocks)
+    for start, stop in chunks(source_ref.shape[1]):
+        for h in range(2):
+            moved = dot(pick, source_ref[h * total : (h + 1) * total, start:stop], ((1,), (0,)))
+            moved = moved.astype(BF16)
+            for j in range(blocks):
+                at = j * pieces + h * half
+                rows_ref[at : at + half, start:stop] = moved[j * half : (j + 1) * half]
+
+
+def to_pieces(out_ref, rows_ref, pieces, blocks, spans):
+    half = pieces // 2
+    total = half * blocks
+    pick = pick_rows(total, half)
+    for start, stop in spans:
+        for h in range(2):
+            part = [
+                rows_ref[j * pieces + h * half : j * pieces + (h + 1) * half, start:stop]
+                for j in range(blocks)
+            ]
+            moved = dot(pick, jnp.concatenate(part, axis=0), ((1,), (0,)))
+            out_ref[h * total : (h + 1) * total, start:stop] = moved.astype(BF16)
 
 
 def fold(block, pieces):
@@ -92,19 +117,54 @@
     )
 
 
-def pack_kernel(partner_ref, q_ref, k_ref, g_ref, delta_ref, out_ref, summary_ref, rows_ref):
+def pack_kernel(
+    partner_hbm,
+    q_hbm,
+    k_hbm,
+    g_hbm,
+    delta_hbm,
+    out_ref,
+    summary_ref,
+    rows_ref,
+    partner_ref,
+    q_ref,
+    k_ref,
+    g_ref,
+    delta_ref,
+    sems,
+    small_sems,
+):
     blocks, pieces, block_len = 8, 64, 256
     score_scale = 1.0 / math.sqrt(HALF)
     pool_scale = 1.0 / math.sqrt(block_len)
-
-    def step(j, carry):
-        at = pl.ds(pl.multiple_of(j * block_len, block_len), block_len)
+    copies = []
+    for half in range(2):
+        at = pl.ds(half * blocks // 2 * block_len, blocks // 2 * block_len)
+        pairs = ((k_hbm, k_ref), (q_hbm, q_ref), (g_hbm, g_ref))
+        copies.append(
+            [
+                pltpu.make_async_copy(there.at[at], here.at[at], sems.at[half, i])
+                for i, (there, here) in enumerate(pairs)
+            ]
+        )
+    copies[0] += [
+        pltpu.make_async_copy(delta_hbm, delta_ref, small_sems.at[0]),
+        pltpu.make_async_copy(partner_hbm, partner_ref, small_sems.at[1]),
+    ]
+    for copy in copies[0] + copies[1]:
+        copy.start()
+
+    for j in range(blocks):
+        if j % (blocks // 2) == 0:
+            for copy in copies[j // (blocks // 2)]:
+                copy.wait()
+        at = slice(j * block_len, (j + 1) * block_len)
         qb, kb, gb = q_ref[at, :], k_ref[at, :], g_ref[at, :]
         scores = dot(kb, head_stack(qb, score_scale), ((1,), (1,)))
         top = jnp.max(scores, axis=0, keepdims=True)
         lse = top + jnp.log(jnp.sum(jnp.exp(scores - top), axis=0, keepdims=True))
         summary = jnp.sum(kb.astype(F32), axis=0, keepdims=True) * pool_scale
-        summary_ref[pl.ds(j, 1), :] = summary
+        summary_ref[j : j + 1, :] = summary
         delta = jnp.concatenate([delta_ref[0:1, at], delta_ref[1:2, at]], axis=1)
         stats = jnp.concatenate([to_rows(lse), to_rows(delta)], axis=0)
         parts = jnp.concatenate(split3(stats), axis=0)
@@ -119,38 +179,38 @@
             (place >> 3).astype(F32),
             jnp.where(lane == 1, (place & 7).astype(F32), 0.0),
         )
-        to = pl.ds(pl.multiple_of(j * pieces, pieces), pieces)
+        to = slice(j * pieces, (j + 1) * pieces)
         rows_ref[to, 0:512] = fold(qb, pieces)
         rows_ref[to, 512:1024] = fold(gb, pieces)
         rows_ref[to, 1024:1152] = jnp.concatenate([left, right], axis=1).astype(BF16)
-        return carry
-
-    lax.fori_loop(0, blocks, step, 0, unroll=True)
-    reorder(out_ref, rows_ref, pieces, blocks, False)
-
-
-def partner_pick(tags):
-    rows = tags.shape[0]
-    place = tags[:, HALF : HALF + 1].astype(F32) * 8.0 + tags[:, HALF + 1 : HALF + 2].astype(F32)
-    lane = lax.broadcasted_iota(jnp.int32, (rows, rows), 1).astype(F32)
-    return jnp.where(lane == place, 1.0, 0.0).astype(BF16)
-
-
-def forward_kernel(in_ref, out_ref):
-    pick = partner_pick(in_ref[:, 1024:1152])
+
+    to_pieces(out_ref, rows_ref, pieces, blocks, chunks(1152))
+
+
+def partner_pick(place):
+    rows = place.shape[1]
+    row = lax.broadcasted_iota(jnp.int32, (rows, rows), 0).astype(F32)
+    return jnp.where(row == place, 1.0, 0.0).astype(BF16)
+
+
+def forward_kernel(in_ref, out_ref, place_ref):
+    tags = in_ref[:, 1024:1152].astype(F32).T
+    place = tags[HALF : HALF + 1, :] * 8.0 + tags[HALF + 1 : HALF + 2, :]
+    place_ref[...] = place
+    pick = partner_pick(place)
     for start in range(0, 1152, 256):
         stop = min(1152, start + 256)
-        out_ref[:, start:stop] = dot(pick, in_ref[:, start:stop], ((0,), (0,))).astype(BF16)
-
-
-def backward_kernel(tags_ref, in_ref, out_ref):
-    pick = partner_pick(tags_ref[...])
+        out_ref[:, start:stop] = dot(pick, in_ref[:, start:stop], ((1,), (0,))).astype(BF16)
+
+
+def backward_kernel(place_ref, in_ref, out_ref):
+    pick = partner_pick(place_ref[...])
     for start in (0, 256):
         out_ref[:, start : start + 256] = dot(
-            pick, in_ref[:, start : start + 256], ((1,), (0,))
+            pick, in_ref[:, start : start + 256], ((0,), (0,))
         ).astype(BF16)
     tail = in_ref[:, 512:640]
-    moved = dot(pick, tail, ((1,), (0,)))
+    moved = dot(pick, tail, ((0,), (0,)))
     rows = tail.shape[0]
     total = jnp.sum(tail.astype(F32).reshape(rows // 8, 8, LANES), axis=0)
     lane8 = lax.broadcasted_iota(jnp.int32, (8, LANES), 1)
@@ -180,7 +240,7 @@
 ):
     blocks, pieces, block_len = 8, 64, 256
     score_scale = 1.0 / math.sqrt(HALF)
-    reorder(rows_ref, in_ref, pieces, blocks, True)
+    to_blocks(rows_ref, in_ref, pieces, blocks)
     arrived = []
     for j in range(blocks):
         s = rows_ref[j * pieces + 48 : j * pieces + 64, 1024:1152].astype(F32)[:, :HALF]
@@ -248,7 +308,7 @@
         back_ref[j * pieces + 32 : j * pieces + 48, 512:640] = jnp.concatenate(
             [parts, jnp.zeros((16, HALF), F32)], axis=1
         ).astype(BF16)
-    reorder(out_ref, back_ref, pieces, blocks, False)
+    to_pieces(out_ref, back_ref, pieces, blocks, chunks(640))
     outer = dot(summary_in, sortq_grad, ((0,), (0,)), precision=lax.Precision.HIGHEST)
     lane = lax.broadcasted_iota(jnp.int32, (LANES, LANES), 1)
     row = lax.broadcasted_iota(jnp.int32, (LANES, LANES), 0)
@@ -273,17 +333,20 @@
     dk_far_ref,
     dv_far_ref,
     column_ref,
+    dq_hbm,
+    dk_hbm,
+    dv_hbm,
+    sort_out,
+    rows_ref,
     dq_out,
     dk_out,
     dv_out,
-    sort_out,
-    rows_ref,
-    extra_ref,
+    sems,
 ):
     blocks, pieces, block_len = 8, 64, 256
     score_scale = 1.0 / math.sqrt(HALF)
     pool_scale = 1.0 / math.sqrt(block_len)
-    reorder(rows_ref, in_ref, pieces, blocks, True)
+    to_blocks(rows_ref, in_ref, pieces, blocks)
     arrived = []
     for j in range(blocks):
         s = rows_ref[j * pieces + 32 : j * pieces + 48, 512:640].astype(F32)[:, :HALF]
@@ -292,7 +355,7 @@
     row_grad = dot(
         sortq_grad, block_diagonal(w_ref), ((1,), (1,)), precision=lax.Precision.HIGHEST
     )
-    extra_ref[...] = pool_scale * (row_grad + column_ref[...])
+    extra = pool_scale * (row_grad + column_ref[...])
 
     lane = lax.broadcasted_iota(jnp.int32, (LANES, LANES), 1)
     found = jnp.zeros((LANES, LANES), F32)
@@ -303,9 +366,10 @@
         found = found + jnp.where((lane >= 16 * a) & (lane < 16 * a + 16), s, 0.0)
     sort_out[...] = found[:, :HALF]
 
-    def step(j, carry):
-        at = pl.ds(pl.multiple_of(j * block_len, block_len), block_len)
-        here = pl.ds(pl.multiple_of(j * pieces, pieces), pieces)
+    copies = []
+    for j in range(blocks):
+        at = slice(j * block_len, (j + 1) * block_len)
+        here = slice(j * pieces, (j + 1) * pieces)
         kb, vb = k_ref[at, :], v_ref[at, :]
         qs = head_stack(q_ref[at, :], score_scale)
         gs = head_stack(g_ref[at, :], 1.0)
@@ -319,9 +383,7 @@
         dprobs = dot(vb, gs, ((1,), (1,)))
         dscores = (probs * (dprobs - delta)).astype(BF16)
         dk = dot(dscores, qs, ((1,), (0,)))
-        dk_out[at, :] = (
-            dk + dk_far_ref[at, :].astype(F32) + extra_ref[pl.ds(j, 1), :]
-        ).astype(BF16)
+        dk_out[at, :] = (dk + dk_far_ref[at, :].astype(F32) + extra[j : j + 1, :]).astype(BF16)
         dv = dot(low, gs, ((1,), (0,)))
         dv_out[at, :] = (dv + dv_far_ref[at, :].astype(F32)).astype(BF16)
         dq = dot(kb, dscores, ((0,), (0,))) * score_scale
@@ -333,26 +395,36 @@
             axis=0,
         )
         dq_out[at, :] = dq.T.astype(BF16)
-        return carry
-
-    lax.fori_loop(0, blocks, step, 0, unroll=True)
+        if j % (blocks // 2) == blocks // 2 - 1:
+            half = j // (blocks // 2)
+            rows = pl.ds(half * blocks // 2 * block_len, blocks // 2 * block_len)
+            pairs = ((dq_out, dq_hbm), (dk_out, dk_hbm), (dv_out, dv_hbm))
+            for i, (here_ref, there) in enumerate(pairs):
+                copy = pltpu.make_async_copy(here_ref.at[rows], there.at[rows], sems.at[half, i])
+                copy.start()
+                copies.append(copy)
+
+    for copy in copies:
+        copy.wait()
 
 
 def whole(memory_space=pltpu.VMEM):
     return pl.BlockSpec(memory_space=memory_space)
 
 
-def call(kernel, outs, inputs, scratch=(), specs=None, flops=1 << 28):
+def call(
+    kernel, outs, inputs, scratch=(), in_hbm=False, out_hbm=0, limit=VMEM_LIMIT, flops=1 << 28
+):
     shapes = [jax.ShapeDtypeStruct(shape, dtype) for shape, dtype in outs]
     size = sum(math.prod(s.shape) * s.dtype.itemsize for s in shapes)
     size += sum(x.size * x.dtype.itemsize for x in inputs)
     return pl.pallas_call(
         kernel,
         out_shape=shapes,
-        in_specs=specs or [whole()] * len(inputs),
-        out_specs=[whole()] * len(shapes),
+        in_specs=[whole(pl.ANY if in_hbm else pltpu.VMEM)] * len(inputs),
+        out_specs=[whole(pl.ANY)] * out_hbm + [whole()] * (len(shapes) - out_hbm),
         scratch_shapes=list(scratch),
-        compiler_params=pltpu.CompilerParams(vmem_limit_bytes=VMEM_LIMIT),
+        compiler_params=pltpu.CompilerParams(vmem_limit_bytes=limit),
         cost_estimate=pl.CostEstimate(flops=flops, bytes_accessed=size, transcendentals=1 << 20),
     )(*inputs)
 
@@ -364,15 +436,29 @@
 def per_device(queries, keys, values, delta, dout, partner, sort_weight):
     tokens = queries.shape[0]
     rows = lax.axis_size("seq") * partner.shape[0]
+    blocks = partner.shape[0]
+    buffer = pltpu.VMEM((tokens, LANES), BF16)
     sent, summary = call(
         pack_kernel,
-        [((rows, 1152), BF16), ((8, LANES), F32)],
+        [((rows, 1152), BF16), ((blocks, LANES), F32)],
         [partner, queries, keys, dout, delta],
-        scratch=[pltpu.VMEM((rows, 1152), BF16)],
-        specs=[whole(pltpu.SMEM)] + [whole()] * 4,
+        scratch=[
+            pltpu.VMEM((rows, 1152), BF16),
+            pltpu.SMEM((blocks,), jnp.int32),
+            buffer,
+            buffer,
+            buffer,
+            pltpu.VMEM(delta.shape, F32),
+            pltpu.SemaphoreType.DMA((2, 3)),
+            pltpu.SemaphoreType.DMA((2,)),
+        ],
+        in_hbm=True,
+        limit=WHOLE_LIMIT,
     )
     spread = exchange(sent)
-    (moved,) = call(forward_kernel, [((rows, 1152), BF16)], [spread])
+    moved, place = call(
+        forward_kernel, [((rows, 1152), BF16), ((1, rows), F32)], [spread]
+    )
     arrived = exchange(moved)
     back, dk_far, dv_far, column = call(
         far_kernel,
@@ -391,9 +477,7 @@
         ],
     )
     spread_back = exchange(back)
-    (moved_back,) = call(
-        backward_kernel, [((rows, 640), BF16)], [spread[:, 1024:1152], spread_back]
-    )
+    (moved_back,) = call(backward_kernel, [((rows, 640), BF16)], [place, spread_back])
     arrived_back = exchange(moved_back)
     d_queries, d_keys, d_values, d_sort = call(
         self_kernel,
@@ -410,7 +494,14 @@
             dv_far,
             column,
         ],
-        scratch=[pltpu.VMEM((rows, 640), BF16), pltpu.VMEM((8, LANES), F32)],
+        scratch=[
+            pltpu.VMEM((rows, 640), BF16),
+            buffer,
+            buffer,
+            buffer,
+            pltpu.SemaphoreType.DMA((2, 3)),
+        ],
+        out_hbm=3,
     )
     return d_queries, d_keys, d_values, d_sort.reshape(sort_weight.shape)
 

time: 159 us -> 153 us (0.962)
  blocking collectives: 108 us -> 134 us
  waiting for transfers between devices: 19.5 us -> 0 us
  local copies, waits for them, and re-layouts: 6.89 us -> 0.04 us
  starting transfers between devices: 6.19 us -> 0 us
    all_to_all x3 -> x4, blocking collectives: 108 us -> 134 us  [exchange(): return lax.all_to_all(x, 'seq', split_axis=0, concat_axis=0, tiled=True)]
    all_to_all x1 -> x0, waiting for transfers between devices: 19.5 us -> none  [exchange(): return lax.all_to_all(x, 'seq', split_axis=0, concat_axis=0, tiled=True)]
    all_to_all x1 -> x0, starting transfers between devices: 6.19 us -> none  [exchange(): return lax.all_to_all(x, 'seq', split_axis=0, concat_axis=0, tiled=True)]
    unnamed x28 -> x14, local copies, waits for them, and re-layouts: 6.22 us -> 0.04 us
  transfers between devices with their start and end apart: 1 -> 0, of which waited for: 1 -> 0; matrix products, arithmetic and copies ran while one was open for 0% -> 0% of each run, Pallas kernels for 0% -> 0%
where the time goes in v3:
time: 153 us
  blocking collectives  134 us (88%)
  Pallas kernels  17.3 us (11%)
    all_to_all x4, blocking collectives, exchange(): return lax.all_to_all(x, 'seq', split_axis=0, concat_axis=0, tiled=True)  134 us
    pallas_call x5, Pallas kernels, call(): pl.pallas_call(kernel, out_shape=shapes, in_specs=[whole(pl.ANY if in_hbm...  17.3 us

profile of v3, /device:TPU:1, one launch (start us, length us, event | category | flops | bytes accessed | tf_op | source)
XLA Modules:
  0.0 152.5 jit_solution(9022391207825826709)
XLA Ops:
  0.6 4.3 %shard_map.102 = (bf16[512,1152]{1,0:T(8,128)(2,1)}, f32[8,128]{1,0:T(8,128)}) custom-call(s32[8]{0:T(128)} %partner_hbm.1, bf16[2048,128]{1,0:T(8,128)(2,1)} %q_ref.1, bf16[2048,128]{1,0:T(8,128)(2,1)} %k_ref.3, bf16[2048,128]{1,0:T(8,128)(2,1)} %g_ref.1, f32[2,2048]{1,0:T(2,128)} %delta_ref.1), custom_call_target="tpu_custom_call" | custom-call | flops 268435456 | bytes 2773024 | tf_op jit(solution)/shard_map/pallas_call | solution.py:421
  4.9 44.5 %all_to_all.44 = bf16[64,8,1152]{2,1,0:T(8,128)(2,1)S(1)} all-to-all(bf16[64,8,1152]{2,1,0:T(8,128)(2,1)} %bitcast.16), channel_id=1, replica_groups=mesh['seq'=64,'head'=4] {'seq'}, dimensions={0} | all-to-all | bytes 2359296 | tf_op jit(solution)/shard_map/all_to_all | solution.py:433
  49.4 0.9 shard_map.103
  50.3 0.0 copy-start
  50.3 0.0 copy-start.1
  50.4 0.0 copy-start.4
  50.4 0.0 copy-start.6
  50.4 37.5 %all_to_all.45 = bf16[64,8,1152]{2,1,0:T(8,128)(2,1)S(1)} all-to-all(bf16[64,8,1152]{2,1,0:T(8,128)(2,1)S(1)} %bitcast.12), channel_id=1, replica_groups=mesh['seq'=64,'head'=4] {'seq'}, dimensions={0} | all-to-all | bytes 2359296 | tf_op jit(solution)/shard_map/all_to_all | solution.py:433
  87.9 0.0 copy-done
  87.9 0.0 copy-done.1
  87.9 0.0 copy-done.4
  87.9 0.0 copy-done.6
  87.9 6.2 %shard_map.104 = (bf16[512,640]{1,0:T(8,128)(2,1)S(1)}, bf16[2048,128]{1,0:T(8,128)(2,1)S(1)}, bf16[2048,128]{1,0:T(8,128)(2,1)S(1)}, f32[8,128]{1,0:T(8,128)S(1)}) custom-call(bf16[512,1152]{1,0:T(8,128)(2,1)S(1)} %bitcast.9, bf16[2048,128]{1,0:T(8,128)(2,1)S(1)} %copy-done, bf16[2048,128]{1,0:T(8,128)(2,1)S(1)} %copy-done.1, f32[8,128]{1,0:T(8,128)S(1)} %copy-done.6, ...), custom_call_target="tpu_custom_call" | custom-call | flops 268435456 | bytes 3973120 | tf_op jit(solution)/shard_map/pallas_call | solution.py:421
  94.1 26.1 %all_to_all.46 = bf16[64,8,640]{2,1,0:T(8,128)(2,1)S(1)} all-to-all(bf16[64,8,640]{2,1,0:T(8,128)(2,1)S(1)} %bitcast.13), channel_id=1, replica_groups=mesh['seq'=64,'head'=4] {'seq'}, dimensions={0} | all-to-all | bytes 1310720 | tf_op jit(solution)/shard_map/all_to_all | solution.py:433
  120.2 0.0 copy-start.2
  120.2 0.0 copy-start.3
  120.2 0.0 copy-start.5
  120.2 0.6 shard_map.105
  120.8 26.2 %all_to_all.47 = bf16[64,8,640]{2,1,0:T(8,128)(2,1)S(1)} all-to-all(bf16[64,8,640]{2,1,0:T(8,128)(2,1)S(1)} %bitcast.15), channel_id=1, replica_groups=mesh['seq'=64,'head'=4] {'seq'}, dimensions={0} | all-to-all | bytes 1310720 | tf_op jit(solution)/shard_map/all_to_all | solution.py:433
  147.0 0.0 copy-done.2
  147.0 0.0 copy-done.3
  147.0 0.0 copy-done.5
  147.0 5.3 %shard_map.106 = (bf16[2048,128]{1,0:T(8,128)(2,1)}, bf16[2048,128]{1,0:T(8,128)(2,1)}, bf16[2048,128]{1,0:T(8,128)(2,1)}, f32[128,64]{1,0:T(8,128)}) custom-call(bf16[512,640]{1,0:T(8,128)(2,1)S(1)} %bitcast.10, bf16[2048,128]{1,0:T(8,128)(2,1)S(1)} %copy-done.2, bf16[2048,128]{1,0:T(8,128)(2,1)S(1)} %copy-done, bf16[2048,128]{1,0:T(8,128)(2,1)S(1)} %copy-done.1, ...), custom_call_target="tpu_custom_call" | custom-call | flops 268435456 | bytes 5459968 | tf_op jit(solution)/shard_map/pallas_call | solution.py:421
Async XLA Ops:
  50.3 37.5 %copy-start = (bf16[2048,128]{1,0:T(8,128)(2,1)S(1)}, bf16[2048,128]{1,0:T(8,128)(2,1)}, u32[]{:S(2)}) copy-start(bf16[2048,128]{1,0:T(8,128)(2,1)} %k_ref.3) | copy-start | bytes 1572868
  50.3 37.5 %copy-start.1 = (bf16[2048,128]{1,0:T(8,128)(2,1)S(1)}, bf16[2048,128]{1,0:T(8,128)(2,1)}, u32[]{:S(2)}) copy-start(bf16[2048,128]{1,0:T(8,128)(2,1)} %v_ref.3) | copy-start | bytes 1572868
  50.4 37.5 %copy-start.4 = (f32[2,64,64]{2,1,0:T(8,128)S(1)}, f32[2,64,64]{2,1,0:T(8,128)}, u32[]{:S(2)}) copy-start(f32[2,64,64]{2,1,0:T(8,128)} %w_ref.3) | copy-start | bytes 98308
  50.4 37.5 %copy-start.6 = (f32[8,128]{1,0:T(8,128)S(1)}, f32[8,128]{1,0:T(8,128)}, u32[]{:S(2)}) copy-start(f32[8,128]{1,0:T(8,128)} %get-tuple-element.19.summary_ref) | copy-start | bytes 12292
  120.2 26.8 %copy-start.2 = (bf16[2048,128]{1,0:T(8,128)(2,1)S(1)}, bf16[2048,128]{1,0:T(8,128)(2,1)}, u32[]{:S(2)}) copy-start(bf16[2048,128]{1,0:T(8,128)(2,1)} %q_ref.1) | copy-start | bytes 1572868
  120.2 26.8 %copy-start.3 = (bf16[2048,128]{1,0:T(8,128)(2,1)S(1)}, bf16[2048,128]{1,0:T(8,128)(2,1)}, u32[]{:S(2)}) copy-start(bf16[2048,128]{1,0:T(8,128)(2,1)} %g_ref.1) | copy-start | bytes 1572868
  120.2 26.8 %copy-start.5 = (f32[2,2048]{1,0:T(2,128)S(1)}, f32[2,2048]{1,0:T(2,128)}, u32[]{:S(2)}) copy-start(f32[2,2048]{1,0:T(2,128)} %delta_ref.1) | copy-start | bytes 49156

commit v4 on v3

--- a/solution.py
+++ b/solution.py
@@ -12,7 +12,8 @@
 BF16 = jnp.bfloat16
 LANES = 128
 HALF = 64
-SHARE_AT = 64
+QUARTER = 32
+SHARE = 16
 VMEM_LIMIT = 48 * 1024 * 1024
 WHOLE_LIMIT = 62240000
 
@@ -22,11 +23,10 @@
 
 
 def head_stack(x, scale):
-    lane = lax.broadcasted_iota(jnp.int32, x.shape, 1)
-    x32 = x.astype(F32) * scale
-    first = jnp.where(lane < HALF, x32, 0.0)
-    second = jnp.where(lane < HALF, 0.0, x32)
-    return jnp.concatenate([first, second], axis=0).astype(BF16)
+    lane = lax.broadcasted_iota(jnp.int32, (1, LANES), 1)
+    first = jnp.where(lane < HALF, scale, 0.0).astype(BF16)
+    second = jnp.where(lane < HALF, 0.0, scale).astype(BF16)
+    return jnp.concatenate([x * first, x * second], axis=0)
 
 
 def split3(x):
@@ -50,6 +50,42 @@
 
 def from_head_rows(x):
     return jnp.concatenate([x[0:1, :], x[1:2, :]], axis=1)
+
+
+def narrow(x):
+    return jnp.concatenate([x[:, :QUARTER], x[:, QUARTER:]], axis=0)
+
+
+def widen(x):
+    rows = x.shape[0] // 2
+    return jnp.concatenate([x[:rows], x[rows:]], axis=1)
+
+
+def load_slots(ref, start, stop, step):
+    low = ref[:, :, start:stop].astype(F32)
+    high = ref[:, :, start + step : stop + step].astype(F32)
+    both = jnp.concatenate([low, high], axis=1)
+    return both.reshape(both.shape[0] * 8, stop - start)
+
+
+def load_slot_stats(ref):
+    both = ref[:, :, 1024:1152].astype(F32)
+    both = jnp.concatenate([both, pltpu.roll(both, HALF, 2)], axis=1)
+    return both.reshape(both.shape[0] * 8, LANES)
+
+
+def store_slots(ref, first, rows, start, stop, step):
+    slots = rows.reshape(rows.shape[0] // 8, 8, stop - start)
+    at = slice(first, first + slots.shape[0])
+    ref[at, :, start:stop] = slots[:, :4].astype(BF16)
+    ref[at, :, start + step : stop + step] = slots[:, 4:].astype(BF16)
+
+
+def store_slot_stats(ref, first, rows):
+    slots = rows.reshape(rows.shape[0] // 8, 8, LANES)
+    lane = lax.broadcasted_iota(jnp.int32, (slots.shape[0], 4, LANES), 2)
+    both = jnp.where(lane < HALF, slots[:, :4], pltpu.roll(slots[:, 4:], HALF, 2))
+    ref[first : first + slots.shape[0], :, 1024:1152] = both.astype(BF16)
 
 
 def block_diagonal(w_ref):
@@ -91,18 +127,13 @@
                 rows_ref[at : at + half, start:stop] = moved[j * half : (j + 1) * half]
 
 
-def to_pieces(out_ref, rows_ref, pieces, blocks, spans):
+def half_to_pieces(pick, rows_ref, pieces, blocks, h, start, stop):
     half = pieces // 2
-    total = half * blocks
-    pick = pick_rows(total, half)
-    for start, stop in spans:
-        for h in range(2):
-            part = [
-                rows_ref[j * pieces + h * half : j * pieces + (h + 1) * half, start:stop]
-                for j in range(blocks)
-            ]
-            moved = dot(pick, jnp.concatenate(part, axis=0), ((1,), (0,)))
-            out_ref[h * total : (h + 1) * total, start:stop] = moved.astype(BF16)
+    part = [
+        rows_ref[j * pieces + h * half : j * pieces + (h + 1) * half, start:stop]
+        for j in range(blocks)
+    ]
+    return dot(pick, jnp.concatenate(part, axis=0), ((1,), (0,)))
 
 
 def fold(block, pieces):
@@ -184,7 +215,11 @@
         rows_ref[to, 512:1024] = fold(gb, pieces)
         rows_ref[to, 1024:1152] = jnp.concatenate([left, right], axis=1).astype(BF16)
 
-    to_pieces(out_ref, rows_ref, pieces, blocks, chunks(1152))
+    pick = pick_rows(rows_ref.shape[0] // 2, pieces // 2)
+    for start, stop in chunks(1152):
+        for h in range(2):
+            moved = half_to_pieces(pick, rows_ref, pieces, blocks, h, start, stop)
+            out_ref[h * 256 : (h + 1) * 256, start:stop] = moved.astype(BF16)
 
 
 def partner_pick(place):
@@ -205,22 +240,21 @@
 
 def backward_kernel(place_ref, in_ref, out_ref):
     pick = partner_pick(place_ref[...])
+    rows = pick.shape[0]
     for start in (0, 256):
-        out_ref[:, start : start + 256] = dot(
-            pick, in_ref[:, start : start + 256], ((0,), (0,))
-        ).astype(BF16)
-    tail = in_ref[:, 512:640]
-    moved = dot(pick, tail, ((0,), (0,)))
-    rows = tail.shape[0]
-    total = jnp.sum(tail.astype(F32).reshape(rows // 8, 8, LANES), axis=0)
+        part = load_slots(in_ref, start, start + 256, 512).astype(BF16)
+        store_slots(out_ref, 0, dot(pick, part, ((0,), (0,))), start, start + 256, 512)
+    tail = load_slot_stats(in_ref)
+    moved = dot(pick, tail.astype(BF16), ((0,), (0,)))
+    total = jnp.sum(tail.reshape(rows // 8, 8, LANES), axis=0)
     lane8 = lax.broadcasted_iota(jnp.int32, (8, LANES), 1)
-    total = total + pltpu.roll(total, LANES - 16, 1) + pltpu.roll(total, LANES - 32, 1)
-    total = jnp.where((lane8 >= SHARE_AT) & (lane8 < SHARE_AT + 16), total, 0.0)
-    high, mid, low = split3(total)
-    share = high + pltpu.roll(mid, 16, 1) + pltpu.roll(low, 32, 1)
+    total = total + pltpu.roll(total, LANES - SHARE, 1)
+    total = jnp.where((lane8 >= QUARTER) & (lane8 < QUARTER + SHARE), total, 0.0)
+    high, mid, _ = split3(total)
+    share = high + pltpu.roll(mid, SHARE, 1)
     share = jnp.broadcast_to(share[None], (rows // 8, 8, LANES)).reshape(rows, LANES)
     lane = lax.broadcasted_iota(jnp.int32, (rows, LANES), 1)
-    out_ref[:, 512:640] = jnp.where(lane < SHARE_AT, moved, share).astype(BF16)
+    store_slot_stats(out_ref, 0, jnp.where(lane < QUARTER, moved, share))
 
 
 def far_kernel(
@@ -277,49 +311,53 @@
         lse = top + jnp.log(total)
         low = probs.astype(BF16)
         dprobs = dot(vb, gs, ((1,), (1,)))
-        gate_terms = jnp.sum(low.astype(F32) * dprobs, axis=0, keepdims=True)
-        first = jnp.sum(gate_terms[:, :block_len], axis=1, keepdims=True)
-        second = jnp.sum(gate_terms[:, block_len:], axis=1, keepdims=True)
-        lane = lax.broadcasted_iota(jnp.int32, (1, LANES), 1)
-        grad_ref[pl.ds(j, 1), :] = jnp.where(lane < HALF, first, second)
         dscores = (probs * (gate_row * dprobs - delta)).astype(BF16)
         dk_ref[at, :] = dot(dscores, qs, ((1,), (0,))).astype(BF16)
-        dv_ref[at, :] = (dot(low, gs, ((1,), (0,))) * gate).astype(BF16)
+        dv = dot(low, gs, ((1,), (0,)))
+        dv_ref[at, :] = (dv * gate).astype(BF16)
+        grad_ref[pl.ds(j, 1), :] = jnp.sum(dv * vb.astype(F32), axis=0, keepdims=True)
         dq = dot(kb, dscores, ((0,), (0,))) * score_scale
         dq = jnp.concatenate([dq[:HALF, :block_len], dq[HALF:, block_len:]], axis=1)
         back_ref[here, 0:512] = dq.astype(BF16)
         parts = jnp.concatenate(
-            list(split3(to_rows(lse))) + [jnp.zeros((pieces - 24, HALF), F32)], axis=0
+            list(split3(narrow(to_rows(lse)))) + [jnp.zeros((16, QUARTER), F32)], axis=0
         )
         back_ref[here, 512:640] = jnp.concatenate(
-            [parts, jnp.zeros((pieces, HALF), F32)], axis=1
+            [parts, jnp.zeros((pieces, LANES - QUARTER), F32)], axis=1
         ).astype(BF16)
         return carry
 
     lax.fori_loop(0, blocks, step, 0, unroll=True)
-    logit_grad = grad_ref[...] * gates * (1.0 - gates)
+    logit_grad = head_sums(grad_ref[...]) * gates * (1.0 - gates)
     sortq_grad = score_scale * logit_grad * summary
     column_ref[...] = score_scale * logit_grad * sortq
     for j in range(blocks):
         parts = jnp.concatenate(
-            list(split3(head_rows(sortq_grad[j : j + 1, :]))) + [jnp.zeros((10, HALF), F32)],
+            list(split3(narrow(head_rows(sortq_grad[j : j + 1, :]))))
+            + [jnp.zeros((4, QUARTER), F32)],
             axis=0,
         )
-        back_ref[j * pieces + 32 : j * pieces + 48, 512:640] = jnp.concatenate(
-            [parts, jnp.zeros((16, HALF), F32)], axis=1
+        back_ref[j * pieces + 48 : (j + 1) * pieces, 512:640] = jnp.concatenate(
+            [parts, jnp.zeros((16, LANES - QUARTER), F32)], axis=1
         ).astype(BF16)
-    to_pieces(out_ref, back_ref, pieces, blocks, chunks(640))
     outer = dot(summary_in, sortq_grad, ((0,), (0,)), precision=lax.Precision.HIGHEST)
     lane = lax.broadcasted_iota(jnp.int32, (LANES, LANES), 1)
     row = lax.broadcasted_iota(jnp.int32, (LANES, LANES), 0)
     outer = jnp.where(row < HALF, outer, pltpu.roll(outer, HALF, 1))
-    inside = (lane >= SHARE_AT) & (lane < SHARE_AT + 16)
+    inside = (lane >= QUARTER) & (lane < QUARTER + SHARE)
+    shares = []
     for a in range(4):
-        part = jnp.where(inside, pltpu.roll(outer, (SHARE_AT - 16 * a) % LANES, 1), 0.0)
-        high, mid, low = split3(part)
-        share = high + pltpu.roll(mid, 16, 1) + pltpu.roll(low, 32, 1)
-        rows = slice(a * LANES, (a + 1) * LANES)
-        out_ref[rows, 512:640] = (out_ref[rows, 512:640].astype(F32) + share).astype(BF16)
+        part = jnp.where(inside, pltpu.roll(outer, (QUARTER - SHARE * a) % LANES, 1), 0.0)
+        high, mid, _ = split3(part)
+        shares.append(high + pltpu.roll(mid, SHARE, 1))
+    pick = pick_rows(rows_ref.shape[0] // 2, pieces // 2)
+    for h in range(2):
+        for start in (0, 256):
+            moved = half_to_pieces(pick, back_ref, pieces, blocks, h, start, start + 256)
+            store_slots(out_ref, h * pieces // 2, moved, start, start + 256, 512)
+        moved = half_to_pieces(pick, back_ref, pieces, blocks, h, 512, 640)
+        moved = moved + jnp.concatenate(shares[2 * h : 2 * h + 2], axis=0)
+        store_slot_stats(out_ref, h * pieces // 2, moved)
 
 
 def self_kernel(
@@ -342,15 +380,20 @@
     dk_out,
     dv_out,
     sems,
+    natural_ref,
 ):
     blocks, pieces, block_len = 8, 64, 256
     score_scale = 1.0 / math.sqrt(HALF)
     pool_scale = 1.0 / math.sqrt(block_len)
-    to_blocks(rows_ref, in_ref, pieces, blocks)
+    for start in (0, 256):
+        part = load_slots(in_ref, start, start + 256, 512)
+        natural_ref[:, start : start + 256] = part.astype(BF16)
+    natural_ref[:, 512:640] = load_slot_stats(in_ref).astype(BF16)
+    to_blocks(rows_ref, natural_ref, pieces, blocks)
     arrived = []
     for j in range(blocks):
-        s = rows_ref[j * pieces + 32 : j * pieces + 48, 512:640].astype(F32)[:, :HALF]
-        arrived.append(from_head_rows(s[0:2] + s[2:4] + s[4:6]))
+        s = rows_ref[j * pieces + 48 : (j + 1) * pieces, 512:640].astype(F32)[:, :QUARTER]
+        arrived.append(from_head_rows(widen(s[0:4] + s[4:8] + s[8:12])))
     sortq_grad = jnp.concatenate(arrived, axis=0)
     row_grad = dot(
         sortq_grad, block_diagonal(w_ref), ((1,), (1,)), precision=lax.Precision.HIGHEST
@@ -360,10 +403,11 @@
     lane = lax.broadcasted_iota(jnp.int32, (LANES, LANES), 1)
     found = jnp.zeros((LANES, LANES), F32)
     for a in range(4):
-        s = in_ref[a * LANES : (a + 1) * LANES, 512:640].astype(F32)
-        s = s + pltpu.roll(s, LANES - 16, 1) + pltpu.roll(s, LANES - 32, 1)
-        s = pltpu.roll(s, (16 * a - SHARE_AT) % LANES, 1)
-        found = found + jnp.where((lane >= 16 * a) & (lane < 16 * a + 16), s, 0.0)
+        s = natural_ref[a * LANES : (a + 1) * LANES, 512:640].astype(F32)
+        s = s + pltpu.roll(s, LANES - SHARE, 1)
+        s = pltpu.roll(s, (SHARE * a - QUARTER) % LANES, 1)
+        inside = (lane >= SHARE * a) & (lane < SHARE * (a + 1))
+        found = found + jnp.where(inside, s, 0.0)
     sort_out[...] = found[:, :HALF]
 
     copies = []
@@ -375,7 +419,8 @@
         gs = head_stack(g_ref[at, :], 1.0)
         far = rows_ref[here, 0:512].astype(F32)
         stats = rows_ref[here, 512:640].astype(F32)
-        lse = from_rows(stats[0:8, :HALF] + stats[8:16, :HALF] + stats[16:24, :HALF])
+        stats = stats[:, :QUARTER]
+        lse = from_rows(widen(stats[0:16] + stats[16:32] + stats[32:48]))
         delta = jnp.concatenate([delta_ref[0:1, at], delta_ref[1:2, at]], axis=1)
         scores = dot(kb, qs, ((1,), (1,)))
         probs = jnp.exp(scores - lse)
@@ -460,10 +505,11 @@
         forward_kernel, [((rows, 1152), BF16), ((1, rows), F32)], [spread]
     )
     arrived = exchange(moved)
+    slots = ((rows // blocks, 4, 1152), BF16)
     back, dk_far, dv_far, column = call(
         far_kernel,
         [
-            ((rows, 640), BF16),
+            slots,
             ((tokens, LANES), BF16),
             ((tokens, LANES), BF16),
             ((8, LANES), F32),
@@ -477,7 +523,7 @@
         ],
     )
     spread_back = exchange(back)
-    (moved_back,) = call(backward_kernel, [((rows, 640), BF16)], [place, spread_back])
+    (moved_back,) = call(backward_kernel, [slots], [place, spread_back])
     arrived_back = exchange(moved_back)
     d_queries, d_keys, d_values, d_sort = call(
         self_kernel,
@@ -500,6 +546,7 @@
             buffer,
             buffer,
             pltpu.SemaphoreType.DMA((2, 3)),
+            pltpu.VMEM((rows, 640), BF16),
         ],
         out_hbm=3,
     )

time: 153 us -> 150 us (0.980)
  blocking collectives: 134 us -> 132 us
    all_to_all x4, blocking collectives: 134 us -> 132 us  [exchange(): return lax.all_to_all(x, 'seq', split_axis=0, concat_axis=0, tiled=True)]
where the time goes in v4:
time: 150 us
  blocking collectives  132 us (88%)
  Pallas kernels  17.2 us (11%)
    all_to_all x4, blocking collectives, exchange(): return lax.all_to_all(x, 'seq', split_axis=0, concat_axis=0, tiled=True)  132 us
    pallas_call x5, Pallas kernels, call(): pl.pallas_call(kernel, out_shape=shapes, in_specs=[whole(pl.ANY if in_hbm...  17.2 us

profile of v4, /device:TPU:1, one launch (start us, length us, event | category | flops | bytes accessed | tf_op | source)
XLA Modules:
  0.0 149.8 jit_solution(17692081183128447667)
XLA Ops:
  0.6 4.3 %shard_map.102 = (bf16[512,1152]{1,0:T(8,128)(2,1)}, f32[8,128]{1,0:T(8,128)}) custom-call(s32[8]{0:T(128)} %partner_hbm.1, bf16[2048,128]{1,0:T(8,128)(2,1)} %q_ref.1, bf16[2048,128]{1,0:T(8,128)(2,1)} %k_ref.3, bf16[2048,128]{1,0:T(8,128)(2,1)} %g_ref.1, f32[2,2048]{1,0:T(2,128)} %delta_ref.1), custom_call_target="tpu_custom_call" | custom-call | flops 268435456 | bytes 2773024 | tf_op jit(solution)/shard_map/pallas_call | solution.py:466
  4.9 44.5 %all_to_all.32 = bf16[64,8,1152]{2,1,0:T(8,128)(2,1)S(1)} all-to-all(bf16[64,8,1152]{2,1,0:T(8,128)(2,1)} %bitcast.8), channel_id=1, replica_groups=mesh['seq'=64,'head'=4] {'seq'}, dimensions={0} | all-to-all | bytes 2359296 | tf_op jit(solution)/shard_map/all_to_all | solution.py:478
  49.4 0.9 shard_map.103
  50.3 0.0 copy-start
  50.4 0.0 copy-start.1
  50.4 0.0 copy-start.4
  50.4 0.0 copy-start.6
  50.4 37.5 %all_to_all.33 = bf16[64,8,1152]{2,1,0:T(8,128)(2,1)S(1)} all-to-all(bf16[64,8,1152]{2,1,0:T(8,128)(2,1)S(1)} %bitcast.7), channel_id=1, replica_groups=mesh['seq'=64,'head'=4] {'seq'}, dimensions={0} | all-to-all | bytes 2359296 | tf_op jit(solution)/shard_map/all_to_all | solution.py:478
  87.9 0.0 copy-done
  87.9 0.0 copy-done.1
  87.9 0.0 copy-done.4
  87.9 0.0 copy-done.6
  87.9 5.8 %shard_map.104 = (bf16[64,4,1152]{2,1,0:T(4,128)(2,1)S(1)}, bf16[2048,128]{1,0:T(8,128)(2,1)S(1)}, bf16[2048,128]{1,0:T(8,128)(2,1)S(1)}, f32[8,128]{1,0:T(8,128)S(1)}) custom-call(bf16[512,1152]{1,0:T(8,128)(2,1)S(1)} %bitcast.5, bf16[2048,128]{1,0:T(8,128)(2,1)S(1)} %copy-done, bf16[2048,128]{1,0:T(8,128)(2,1)S(1)} %copy-done.1, f32[8,128]{1,0:T(8,128)S(1)} %copy-done.6, ...), custom_call_target="tpu_custom_call" | custom-call | flops 268435456 | bytes 3907584 | tf_op jit(solution)/shard_map/pallas_call | solution.py:466
  93.7 24.7 %all_to_all.34.in_ref = bf16[64,4,1152]{2,1,0:T(4,128)(2,1)S(1)} all-to-all(bf16[64,4,1152]{2,1,0:T(4,128)(2,1)S(1)} %get-tuple-element.20), channel_id=1, replica_groups=mesh['seq'=64,'head'=4] {'seq'}, dimensions={0} | all-to-all | bytes 1179648 | tf_op jit(solution)/shard_map/all_to_all | solution.py:478
  118.4 0.0 copy-start.2
  118.4 0.0 copy-start.3
  118.4 0.0 copy-start.5
  118.4 0.8 shard_map.105
  119.2 25.0 %all_to_all.35.in_ref = bf16[64,4,1152]{2,1,0:T(4,128)(2,1)S(1)} all-to-all(bf16[64,4,1152]{2,1,0:T(4,128)(2,1)S(1)} %shard_map.105), channel_id=1, replica_groups=mesh['seq'=64,'head'=4] {'seq'}, dimensions={0} | all-to-all | bytes 1179648 | tf_op jit(solution)/shard_map/all_to_all | solution.py:478
  144.1 0.0 copy-done.2
  144.2 0.0 copy-done.3
  144.2 0.0 copy-done.5
  144.2 5.5 %shard_map.106 = (bf16[2048,128]{1,0:T(8,128)(2,1)}, bf16[2048,128]{1,0:T(8,128)(2,1)}, bf16[2048,128]{1,0:T(8,128)(2,1)}, f32[128,64]{1,0:T(8,128)}) custom-call(bf16[64,4,1152]{2,1,0:T(4,128)(2,1)S(1)} %all_to_all.35.in_ref, bf16[2048,128]{1,0:T(8,128)(2,1)S(1)} %copy-done.2, bf16[2048,128]{1,0:T(8,128)(2,1)S(1)} %copy-done, ...), custom_call_target="tpu_custom_call" | custom-call | flops 268435456 | bytes 5394432 | tf_op jit(solution)/shard_map/pallas_call | solution.py:466
Async XLA Ops:
  50.3 37.5 %copy-start = (bf16[2048,128]{1,0:T(8,128)(2,1)S(1)}, bf16[2048,128]{1,0:T(8,128)(2,1)}, u32[]{:S(2)}) copy-start(bf16[2048,128]{1,0:T(8,128)(2,1)} %k_ref.3) | copy-start | bytes 1572868
  50.4 37.5 %copy-start.1 = (bf16[2048,128]{1,0:T(8,128)(2,1)S(1)}, bf16[2048,128]{1,0:T(8,128)(2,1)}, u32[]{:S(2)}) copy-start(bf16[2048,128]{1,0:T(8,128)(2,1)} %v_ref.3) | copy-start | bytes 1572868
  50.4 37.5 %copy-start.4 = (f32[2,64,64]{2,1,0:T(8,128)S(1)}, f32[2,64,64]{2,1,0:T(8,128)}, u32[]{:S(2)}) copy-start(f32[2,64,64]{2,1,0:T(8,128)} %w_ref.3) | copy-start | bytes 98308
  50.4 37.5 %copy-start.6 = (f32[8,128]{1,0:T(8,128)S(1)}, f32[8,128]{1,0:T(8,128)}, u32[]{:S(2)}) copy-start(f32[8,128]{1,0:T(8,128)} %get-tuple-element.19.summary_ref) | copy-start | bytes 12292
  118.4 25.7 %copy-start.2 = (bf16[2048,128]{1,0:T(8,128)(2,1)S(1)}, bf16[2048,128]{1,0:T(8,128)(2,1)}, u32[]{:S(2)}) copy-start(bf16[2048,128]{1,0:T(8,128)(2,1)} %q_ref.1) | copy-start | bytes 1572868
  118.4 25.7 %copy-start.3 = (bf16[2048,128]{1,0:T(8,128)(2,1)S(1)}, bf16[2048,128]{1,0:T(8,128)(2,1)}, u32[]{:S(2)}) copy-start(bf16[2048,128]{1,0:T(8,128)(2,1)} %g_ref.1) | copy-start | bytes 1572868
  118.4 25.7 %copy-start.5 = (f32[2,2048]{1,0:T(2,128)S(1)}, f32[2,2048]{1,0:T(2,128)}, u32[]{:S(2)}) copy-start(f32[2,2048]{1,0:T(2,128)} %delta_ref.1) | copy-start | bytes 49156

commit v5 on v4

--- a/solution.py
+++ b/solution.py
@@ -14,6 +14,7 @@
 HALF = 64
 QUARTER = 32
 SHARE = 16
+TAGS = 48
 VMEM_LIMIT = 48 * 1024 * 1024
 WHOLE_LIMIT = 62240000
 
@@ -53,7 +54,8 @@
 
 
 def narrow(x):
-    return jnp.concatenate([x[:, :QUARTER], x[:, QUARTER:]], axis=0)
+    width = x.shape[1] // 2
+    return jnp.concatenate([x[:, :width], x[:, width:]], axis=0)
 
 
 def widen(x):
@@ -61,31 +63,25 @@
     return jnp.concatenate([x[:rows], x[rows:]], axis=1)
 
 
-def load_slots(ref, start, stop, step):
-    low = ref[:, :, start:stop].astype(F32)
-    high = ref[:, :, start + step : stop + step].astype(F32)
-    both = jnp.concatenate([low, high], axis=1)
-    return both.reshape(both.shape[0] * 8, stop - start)
-
-
-def load_slot_stats(ref):
-    both = ref[:, :, 1024:1152].astype(F32)
-    both = jnp.concatenate([both, pltpu.roll(both, HALF, 2)], axis=1)
-    return both.reshape(both.shape[0] * 8, LANES)
-
-
-def store_slots(ref, first, rows, start, stop, step):
-    slots = rows.reshape(rows.shape[0] // 8, 8, stop - start)
-    at = slice(first, first + slots.shape[0])
-    ref[at, :, start:stop] = slots[:, :4].astype(BF16)
-    ref[at, :, start + step : stop + step] = slots[:, 4:].astype(BF16)
-
-
-def store_slot_stats(ref, first, rows):
-    slots = rows.reshape(rows.shape[0] // 8, 8, LANES)
-    lane = lax.broadcasted_iota(jnp.int32, (slots.shape[0], 4, LANES), 2)
-    both = jnp.where(lane < HALF, slots[:, :4], pltpu.roll(slots[:, 4:], HALF, 2))
-    ref[first : first + slots.shape[0], :, 1024:1152] = both.astype(BF16)
+def load_half(ref, half, start, stop, step):
+    part = ref[:, :, start + half * step : stop + half * step].astype(F32)
+    return part.reshape(part.shape[0] * 4, stop - start).astype(BF16)
+
+
+def load_half_stats(ref, half, at):
+    part = ref[:, :, at : at + LANES].astype(F32).reshape(ref.shape[0] * 4, LANES)
+    return pltpu.roll(part, HALF, 1) if half else part
+
+
+def store_half(ref, half, rows, start, stop, step):
+    slots = rows.reshape(ref.shape[0], 4, stop - start).astype(BF16)
+    ref[:, :, start + half * step : stop + half * step] = slots
+
+
+def store_stats(ref, at, low, high):
+    lane = lax.broadcasted_iota(jnp.int32, low.shape, 1)
+    both = jnp.where(lane < HALF, low, pltpu.roll(high, HALF, 1))
+    ref[:, :, at : at + LANES] = both.reshape(ref.shape[0], 4, LANES).astype(BF16)
 
 
 def block_diagonal(w_ref):
@@ -111,29 +107,37 @@
 
 
 def chunks(width):
-    return [(start, min(width, start + 256)) for start in range(0, width, 256)]
-
-
-def to_blocks(rows_ref, source_ref, pieces, blocks):
-    half = pieces // 2
-    total = half * blocks
-    pick = pick_rows(total, blocks)
-    for start, stop in chunks(source_ref.shape[1]):
-        for h in range(2):
-            moved = dot(pick, source_ref[h * total : (h + 1) * total, start:stop], ((1,), (0,)))
-            moved = moved.astype(BF16)
-            for j in range(blocks):
-                at = j * pieces + h * half
-                rows_ref[at : at + half, start:stop] = moved[j * half : (j + 1) * half]
-
-
-def half_to_pieces(pick, rows_ref, pieces, blocks, h, start, stop):
-    half = pieces // 2
-    part = [
-        rows_ref[j * pieces + h * half : j * pieces + (h + 1) * half, start:stop]
-        for j in range(blocks)
-    ]
-    return dot(pick, jnp.concatenate(part, axis=0), ((1,), (0,)))
+    return [(start, start + 256) for start in range(0, width, 256)]
+
+
+def send_rows(out_ref, rows_ref, width, extra):
+    half_rows = rows_ref.shape[0] // 2
+    pick = pick_rows(half_rows, half_rows // 4)
+    tails = []
+    for h in range(2):
+        at = slice(h * half_rows, (h + 1) * half_rows)
+        for start, stop in chunks(width):
+            moved = dot(pick, rows_ref[at, start:stop], ((1,), (0,)))
+            store_half(out_ref, h, moved, start, stop, width)
+        tails.append(dot(pick, rows_ref[at, width : width + LANES], ((1,), (0,))))
+        if extra is not None:
+            tails[h] = tails[h] + extra[h]
+    store_stats(out_ref, 2 * width, *tails)
+
+
+def receive_rows(rows_ref, in_ref, width):
+    half_rows = rows_ref.shape[0] // 2
+    pick = pick_rows(half_rows, 4)
+    tails = []
+    for h in range(2):
+        at = slice(h * half_rows, (h + 1) * half_rows)
+        for start, stop in chunks(width):
+            part = load_half(in_ref, h, start, stop, width)
+            rows_ref[at, start:stop] = dot(pick, part, ((1,), (0,))).astype(BF16)
+        tails.append(load_half_stats(in_ref, h, 2 * width))
+        moved = dot(pick, tails[h].astype(BF16), ((1,), (0,)))
+        rows_ref[at, width : width + LANES] = moved.astype(BF16)
+    return tails
 
 
 def fold(block, pieces):
@@ -197,29 +201,27 @@
         summary = jnp.sum(kb.astype(F32), axis=0, keepdims=True) * pool_scale
         summary_ref[j : j + 1, :] = summary
         delta = jnp.concatenate([delta_ref[0:1, at], delta_ref[1:2, at]], axis=1)
-        stats = jnp.concatenate([to_rows(lse), to_rows(delta)], axis=0)
-        parts = jnp.concatenate(split3(stats), axis=0)
-        summary_parts = jnp.concatenate(
-            list(split3(head_rows(summary))) + [jnp.zeros((10, HALF), F32)], axis=0
-        )
-        left = jnp.concatenate([parts, summary_parts], axis=0)
-        lane = lax.broadcasted_iota(jnp.int32, (pieces, HALF), 1)
+        left = jnp.concatenate(
+            list(split3(narrow(to_rows(lse))))
+            + list(split3(narrow(head_rows(summary))))
+            + [jnp.zeros((4, QUARTER), F32)],
+            axis=0,
+        )
+        deltas = jnp.concatenate(split3(narrow(narrow(to_rows(delta))))[:2], axis=0)
+        lane = lax.broadcasted_iota(jnp.int32, (pieces, LANES - TAGS), 1)
         place = partner_ref[j]
-        right = jnp.where(
+        high = ((place & 4) << 4) | (place >> 3)
+        tags = jnp.where(
             lane == 0,
-            (place >> 3).astype(F32),
-            jnp.where(lane == 1, (place & 7).astype(F32), 0.0),
+            high.astype(F32),
+            jnp.where(lane == 1, (place & 3).astype(F32), 0.0),
         )
         to = slice(j * pieces, (j + 1) * pieces)
         rows_ref[to, 0:512] = fold(qb, pieces)
         rows_ref[to, 512:1024] = fold(gb, pieces)
-        rows_ref[to, 1024:1152] = jnp.concatenate([left, right], axis=1).astype(BF16)
-
-    pick = pick_rows(rows_ref.shape[0] // 2, pieces // 2)
-    for start, stop in chunks(1152):
-        for h in range(2):
-            moved = half_to_pieces(pick, rows_ref, pieces, blocks, h, start, stop)
-            out_ref[h * 256 : (h + 1) * 256, start:stop] = moved.astype(BF16)
+        rows_ref[to, 1024:1152] = jnp.concatenate([left, deltas, tags], axis=1).astype(BF16)
+
+    send_rows(out_ref, rows_ref, 1024, None)
 
 
 def partner_pick(place):
@@ -229,32 +231,50 @@
 
 
 def forward_kernel(in_ref, out_ref, place_ref):
-    tags = in_ref[:, 1024:1152].astype(F32).T
-    place = tags[HALF : HALF + 1, :] * 8.0 + tags[HALF + 1 : HALF + 2, :]
+    tail = jnp.concatenate([load_half_stats(in_ref, h, 2048) for h in range(2)], axis=0)
+    tags = tail.T
+    place = tags[TAGS : TAGS + 1, :] * 4.0 + tags[TAGS + 1 : TAGS + 2, :]
     place_ref[...] = place
     pick = partner_pick(place)
-    for start in range(0, 1152, 256):
-        stop = min(1152, start + 256)
-        out_ref[:, start:stop] = dot(pick, in_ref[:, start:stop], ((1,), (0,))).astype(BF16)
+    half_rows = tail.shape[0] // 2
+    for start, stop in chunks(1024):
+        part = jnp.concatenate(
+            [load_half(in_ref, h, start, stop, 1024) for h in range(2)], axis=0
+        )
+        moved = dot(pick, part, ((1,), (0,)))
+        store_half(out_ref, 0, moved[:half_rows], start, stop, 1024)
+        store_half(out_ref, 1, moved[half_rows:], start, stop, 1024)
+    moved = dot(pick, tail.astype(BF16), ((1,), (0,)))
+    store_stats(out_ref, 2048, moved[:half_rows], moved[half_rows:])
 
 
 def backward_kernel(place_ref, in_ref, out_ref):
     pick = partner_pick(place_ref[...])
-    rows = pick.shape[0]
-    for start in (0, 256):
-        part = load_slots(in_ref, start, start + 256, 512).astype(BF16)
-        store_slots(out_ref, 0, dot(pick, part, ((0,), (0,))), start, start + 256, 512)
-    tail = load_slot_stats(in_ref)
-    moved = dot(pick, tail.astype(BF16), ((0,), (0,)))
-    total = jnp.sum(tail.reshape(rows // 8, 8, LANES), axis=0)
+    half_rows = pick.shape[0] // 2
+    for start, stop in chunks(512):
+        part = jnp.concatenate(
+            [load_half(in_ref, h, start, stop, 512) for h in range(2)], axis=0
+        )
+        moved = dot(pick, part, ((0,), (0,)))
+        store_half(out_ref, 0, moved[:half_rows], start, stop, 512)
+        store_half(out_ref, 1, moved[half_rows:], start, stop, 512)
+    tails = [load_half_stats(in_ref, h, 1024) for h in range(2)]
+    moved = dot(pick, jnp.concatenate(tails, axis=0).astype(BF16), ((0,), (0,)))
     lane8 = lax.broadcasted_iota(jnp.int32, (8, LANES), 1)
-    total = total + pltpu.roll(total, LANES - SHARE, 1)
-    total = jnp.where((lane8 >= QUARTER) & (lane8 < QUARTER + SHARE), total, 0.0)
-    high, mid, _ = split3(total)
-    share = high + pltpu.roll(mid, SHARE, 1)
-    share = jnp.broadcast_to(share[None], (rows // 8, 8, LANES)).reshape(rows, LANES)
-    lane = lax.broadcasted_iota(jnp.int32, (rows, LANES), 1)
-    store_slot_stats(out_ref, 0, jnp.where(lane < QUARTER, moved, share))
+    lane = lax.broadcasted_iota(jnp.int32, (half_rows, LANES), 1)
+    sent = []
+    for h in range(2):
+        total = jnp.sum(tails[h].reshape(half_rows // 8, 8, LANES), axis=0)
+        total = total + pltpu.roll(total, 4, 0)
+        total = total + pltpu.roll(total, LANES - SHARE, 1)
+        total = jnp.where((lane8 >= QUARTER) & (lane8 < QUARTER + SHARE), total, 0.0)
+        high, mid, _ = split3(total)
+        share = high + pltpu.roll(mid, SHARE, 1)
+        share = jnp.broadcast_to(share[None], (half_rows // 8, 8, LANES))
+        share = share.reshape(half_rows, LANES)
+        at = slice(h * half_rows, (h + 1) * half_rows)
+        sent.append(jnp.where(lane < QUARTER, moved[at], share))
+    store_stats(out_ref, 1024, *sent)
 
 
 def far_kernel(
@@ -274,11 +294,11 @@
 ):
     blocks, pieces, block_len = 8, 64, 256
     score_scale = 1.0 / math.sqrt(HALF)
-    to_blocks(rows_ref, in_ref, pieces, blocks)
+    receive_rows(rows_ref, in_ref, 1024)
     arrived = []
     for j in range(blocks):
-        s = rows_ref[j * pieces + 48 : j * pieces + 64, 1024:1152].astype(F32)[:, :HALF]
-        arrived.append(from_head_rows(s[0:2] + s[2:4] + s[4:6]))
+        s = rows_ref[j * pieces + 48 : (j + 1) * pieces, 1024:1152].astype(F32)[:, :QUARTER]
+        arrived.append(from_head_rows(widen(s[0:4] + s[4:8] + s[8:12])))
     summary_in = jnp.concatenate(arrived, axis=0)
     summary = summary_ref[...]
     sortq = dot(summary_in, block_diagonal(w_ref), ((1,), (0,)), precision=lax.Precision.HIGHEST)
@@ -292,9 +312,10 @@
         qs = head_stack(unfold(rows_ref[here, 0:512]), score_scale)
         gs = head_stack(unfold(rows_ref[here, 512:1024]), 1.0)
         stats = rows_ref[here, 1024:1152].astype(F32)
-        joined = stats[0:16, :HALF] + stats[16:32, :HALF] + stats[32:48, :HALF]
-        own_lse = from_rows(joined[0:8])
-        delta = from_rows(joined[8:16])
+        parts = stats[:, :QUARTER]
+        own_lse = from_rows(widen(parts[0:16] + parts[16:32] + parts[32:48]))
+        parts = stats[:, QUARTER:TAGS]
+        delta = from_rows(widen(widen(parts[0:32] + parts[32:64])))
         gate = gate_ref[pl.ds(j, 1), :]
         gate_row = jnp.concatenate(
             [
@@ -350,14 +371,8 @@
         part = jnp.where(inside, pltpu.roll(outer, (QUARTER - SHARE * a) % LANES, 1), 0.0)
         high, mid, _ = split3(part)
         shares.append(high + pltpu.roll(mid, SHARE, 1))
-    pick = pick_rows(rows_ref.shape[0] // 2, pieces // 2)
-    for h in range(2):
-        for start in (0, 256):
-            moved = half_to_pieces(pick, back_ref, pieces, blocks, h, start, start + 256)
-            store_slots(out_ref, h * pieces // 2, moved, start, start + 256, 512)
-        moved = half_to_pieces(pick, back_ref, pieces, blocks, h, 512, 640)
-        moved = moved + jnp.concatenate(shares[2 * h : 2 * h + 2], axis=0)
-        store_slot_stats(out_ref, h * pieces // 2, moved)
+    extra = [jnp.concatenate(shares[2 * h : 2 * h + 2], axis=0) for h in range(2)]
+    send_rows(out_ref, back_ref, 512, extra)
 
 
 def self_kernel(
@@ -380,16 +395,11 @@
     dk_out,
     dv_out,
     sems,
-    natural_ref,
 ):
     blocks, pieces, block_len = 8, 64, 256
     score_scale = 1.0 / math.sqrt(HALF)
     pool_scale = 1.0 / math.sqrt(block_len)
-    for start in (0, 256):
-        part = load_slots(in_ref, start, start + 256, 512)
-        natural_ref[:, start : start + 256] = part.astype(BF16)
-    natural_ref[:, 512:640] = load_slot_stats(in_ref).astype(BF16)
-    to_blocks(rows_ref, natural_ref, pieces, blocks)
+    tails = receive_rows(rows_ref, in_ref, 512)
     arrived = []
     for j in range(blocks):
         s = rows_ref[j * pieces + 48 : (j + 1) * pieces, 512:640].astype(F32)[:, :QUARTER]
@@ -403,7 +413,7 @@
     lane = lax.broadcasted_iota(jnp.int32, (LANES, LANES), 1)
     found = jnp.zeros((LANES, LANES), F32)
     for a in range(4):
-        s = natural_ref[a * LANES : (a + 1) * LANES, 512:640].astype(F32)
+        s = tails[a // 2][(a % 2) * LANES : (a % 2 + 1) * LANES]
         s = s + pltpu.roll(s, LANES - SHARE, 1)
         s = pltpu.roll(s, (SHARE * a - QUARTER) % LANES, 1)
         inside = (lane >= SHARE * a) & (lane < SHARE * (a + 1))
@@ -483,9 +493,10 @@
     rows = lax.axis_size("seq") * partner.shape[0]
     blocks = partner.shape[0]
     buffer = pltpu.VMEM((tokens, LANES), BF16)
+    wide_slots = ((rows // blocks, 4, 2176), BF16)
     sent, summary = call(
         pack_kernel,
-        [((rows, 1152), BF16), ((blocks, LANES), F32)],
+        [wide_slots, ((blocks, LANES), F32)],
         [partner, queries, keys, dout, delta],
         scratch=[
             pltpu.VMEM((rows, 1152), BF16),
@@ -502,7 +513,7 @@
     )
     spread = exchange(sent)
     moved, place = call(
-        forward_kernel, [((rows, 1152), BF16), ((1, rows), F32)], [spread]
+        forward_kernel, [wide_slots, ((1, rows), F32)], [spread]
     )
     arrived = exchange(moved)
     slots = ((rows // blocks, 4, 1152), BF16)
@@ -546,7 +557,6 @@
             buffer,
             buffer,
             pltpu.SemaphoreType.DMA((2, 3)),
-            pltpu.VMEM((rows, 640), BF16),
         ],
         out_hbm=3,
     )

time: 150 us -> 147 us (0.980)
  blocking collectives: 132 us -> 129 us
    all_to_all x4, blocking collectives: 132 us -> 129 us  [exchange(): return lax.all_to_all(x, 'seq', split_axis=0, concat_axis=0, tiled=True)]
where the time goes in v5:
time: 147 us
  blocking collectives  129 us (88%)
  Pallas kernels  17.5 us (12%)
    all_to_all x4, blocking collectives, exchange(): return lax.all_to_all(x, 'seq', split_axis=0, concat_axis=0, tiled=True)  129 us
    pallas_call x5, Pallas kernels, call(): pl.pallas_call(kernel, out_shape=shapes, in_specs=[whole(pl.ANY if in_hbm...  17.5 us

profile of v5, /device:TPU:1, one launch (start us, length us, event | category | flops | bytes accessed | tf_op | source)
XLA Modules:
  0.0 147.1 jit_solution(4641309299050183644)
XLA Ops:
  0.6 4.4 %shard_map.102 = (bf16[64,4,2176]{2,1,0:T(4,128)(2,1)}, f32[8,128]{1,0:T(8,128)}) custom-call(s32[8]{0:T(128)} %partner_hbm.1, bf16[2048,128]{1,0:T(8,128)(2,1)} %q_ref.1, bf16[2048,128]{1,0:T(8,128)(2,1)} %k_ref.3, bf16[2048,128]{1,0:T(8,128)(2,1)} %g_ref.1, f32[2,2048]{1,0:T(2,128)} %delta_ref.1), custom_call_target="tpu_custom_call" | custom-call | flops 268435456 | bytes 2707488 | tf_op jit(solution)/shard_map/pallas_call | solution.py:476
  5.0 43.1 %all_to_all.20.in_ref = bf16[64,4,2176]{2,1,0:T(4,128)(2,1)S(1)} all-to-all(bf16[64,4,2176]{2,1,0:T(4,128)(2,1)} %get-tuple-element.16), channel_id=1, replica_groups=mesh['seq'=64,'head'=4] {'seq'}, dimensions={0} | all-to-all | bytes 2228224 | tf_op jit(solution)/shard_map/all_to_all | solution.py:488
  48.1 1.1 shard_map.103
  49.2 0.0 copy-start
  49.2 0.0 copy-start.1
  49.2 0.0 copy-start.4
  49.2 0.0 copy-start.6
  49.3 36.1 %all_to_all.21.in_ref = bf16[64,4,2176]{2,1,0:T(4,128)(2,1)S(1)} all-to-all(bf16[64,4,2176]{2,1,0:T(4,128)(2,1)S(1)} %get-tuple-element.18), channel_id=1, replica_groups=mesh['seq'=64,'head'=4] {'seq'}, dimensions={0} | all-to-all | bytes 2228224 | tf_op jit(solution)/shard_map/all_to_all | solution.py:488
  85.3 0.0 copy-done
  85.3 0.0 copy-done.1
  85.3 0.0 copy-done.4
  85.4 0.0 copy-done.6
  85.4 5.9 %shard_map.104 = (bf16[64,4,1152]{2,1,0:T(4,128)(2,1)S(1)}, bf16[2048,128]{1,0:T(8,128)(2,1)S(1)}, bf16[2048,128]{1,0:T(8,128)(2,1)S(1)}, f32[8,128]{1,0:T(8,128)S(1)}) custom-call(bf16[64,4,2176]{2,1,0:T(4,128)(2,1)S(1)} %all_to_all.21.in_ref, bf16[2048,128]{1,0:T(8,128)(2,1)S(1)} %copy-done, bf16[2048,128]{1,0:T(8,128)(2,1)S(1)} %copy-done.1, ...), custom_call_target="tpu_custom_call" | custom-call | flops 268435456 | bytes 3842048 | tf_op jit(solution)/shard_map/pallas_call | solution.py:476
  91.3 24.7 %all_to_all.22.in_ref = bf16[64,4,1152]{2,1,0:T(4,128)(2,1)S(1)} all-to-all(bf16[64,4,1152]{2,1,0:T(4,128)(2,1)S(1)} %get-tuple-element.20), channel_id=1, replica_groups=mesh['seq'=64,'head'=4] {'seq'}, dimensions={0} | all-to-all | bytes 1179648 | tf_op jit(solution)/shard_map/all_to_all | solution.py:488
  116.0 0.0 copy-start.2
  116.0 0.0 copy-start.3
  116.0 0.0 copy-start.5
  116.0 0.7 shard_map.105
  116.7 24.8 %all_to_all.23.in_ref = bf16[64,4,1152]{2,1,0:T(4,128)(2,1)S(1)} all-to-all(bf16[64,4,1152]{2,1,0:T(4,128)(2,1)S(1)} %shard_map.105), channel_id=1, replica_groups=mesh['seq'=64,'head'=4] {'seq'}, dimensions={0} | all-to-all | bytes 1179648 | tf_op jit(solution)/shard_map/all_to_all | solution.py:488
  141.5 0.0 copy-done.2
  141.5 0.0 copy-done.3
  141.5 0.0 copy-done.5
  141.5 5.5 %shard_map.106 = (bf16[2048,128]{1,0:T(8,128)(2,1)}, bf16[2048,128]{1,0:T(8,128)(2,1)}, bf16[2048,128]{1,0:T(8,128)(2,1)}, f32[128,64]{1,0:T(8,128)}) custom-call(bf16[64,4,1152]{2,1,0:T(4,128)(2,1)S(1)} %all_to_all.23.in_ref, bf16[2048,128]{1,0:T(8,128)(2,1)S(1)} %copy-done.2, bf16[2048,128]{1,0:T(8,128)(2,1)S(1)} %copy-done, ...), custom_call_target="tpu_custom_call" | custom-call | flops 268435456 | bytes 5394432 | tf_op jit(solution)/shard_map/pallas_call | solution.py:476
Async XLA Ops:
  49.2 36.1 %copy-start = (bf16[2048,128]{1,0:T(8,128)(2,1)S(1)}, bf16[2048,128]{1,0:T(8,128)(2,1)}, u32[]{:S(2)}) copy-start(bf16[2048,128]{1,0:T(8,128)(2,1)} %k_ref.3) | copy-start | bytes 1572868
  49.2 36.1 %copy-start.1 = (bf16[2048,128]{1,0:T(8,128)(2,1)S(1)}, bf16[2048,128]{1,0:T(8,128)(2,1)}, u32[]{:S(2)}) copy-start(bf16[2048,128]{1,0:T(8,128)(2,1)} %v_ref.3) | copy-start | bytes 1572868
  49.2 36.1 %copy-start.4 = (f32[2,64,64]{2,1,0:T(8,128)S(1)}, f32[2,64,64]{2,1,0:T(8,128)}, u32[]{:S(2)}) copy-start(f32[2,64,64]{2,1,0:T(8,128)} %w_ref.3) | copy-start | bytes 98308
  49.2 36.1 %copy-start.6 = (f32[8,128]{1,0:T(8,128)S(1)}, f32[8,128]{1,0:T(8,128)}, u32[]{:S(2)}) copy-start(f32[8,128]{1,0:T(8,128)} %get-tuple-element.19.summary_ref) | copy-start | bytes 12292
  116.0 25.5 %copy-start.2 = (bf16[2048,128]{1,0:T(8,128)(2,1)S(1)}, bf16[2048,128]{1,0:T(8,128)(2,1)}, u32[]{:S(2)}) copy-start(bf16[2048,128]{1,0:T(8,128)(2,1)} %q_ref.1) | copy-start | bytes 1572868
  116.0 25.5 %copy-start.3 = (bf16[2048,128]{1,0:T(8,128)(2,1)S(1)}, bf16[2048,128]{1,0:T(8,128)(2,1)}, u32[]{:S(2)}) copy-start(bf16[2048,128]{1,0:T(8,128)(2,1)} %g_ref.1) | copy-start | bytes 1572868
  116.0 25.5 %copy-start.5 = (f32[2,2048]{1,0:T(2,128)S(1)}, f32[2,2048]{1,0:T(2,128)}, u32[]{:S(2)}) copy-start(f32[2,2048]{1,0:T(2,128)} %delta_ref.1) | copy-start | bytes 49156

commit v6 on v5

--- a/solution.py
+++ b/solution.py
@@ -110,18 +110,18 @@
     return [(start, start + 256) for start in range(0, width, 256)]
 
 
-def send_rows(out_ref, rows_ref, width, extra):
+def send_half(out_ref, rows_ref, width, h):
     half_rows = rows_ref.shape[0] // 2
     pick = pick_rows(half_rows, half_rows // 4)
-    tails = []
-    for h in range(2):
-        at = slice(h * half_rows, (h + 1) * half_rows)
-        for start, stop in chunks(width):
-            moved = dot(pick, rows_ref[at, start:stop], ((1,), (0,)))
-            store_half(out_ref, h, moved, start, stop, width)
-        tails.append(dot(pick, rows_ref[at, width : width + LANES], ((1,), (0,))))
-        if extra is not None:
-            tails[h] = tails[h] + extra[h]
+    at = slice(h * half_rows, (h + 1) * half_rows)
+    for start, stop in chunks(width):
+        moved = dot(pick, rows_ref[at, start:stop], ((1,), (0,)))
+        store_half(out_ref, h, moved, start, stop, width)
+    return dot(pick, rows_ref[at, width : width + LANES], ((1,), (0,)))
+
+
+def send_rows(out_ref, rows_ref, width, extra):
+    tails = [send_half(out_ref, rows_ref, width, h) + extra[h] for h in range(2)]
     store_stats(out_ref, 2 * width, *tails)
 
 
@@ -158,8 +158,9 @@
     k_hbm,
     g_hbm,
     delta_hbm,
+    out_hbm,
+    summary_ref,
     out_ref,
-    summary_ref,
     rows_ref,
     partner_ref,
     q_ref,
@@ -168,6 +169,7 @@
     delta_ref,
     sems,
     small_sems,
+    out_sems,
 ):
     blocks, pieces, block_len = 8, 64, 256
     score_scale = 1.0 / math.sqrt(HALF)
@@ -175,13 +177,14 @@
     copies = []
     for half in range(2):
         at = pl.ds(half * blocks // 2 * block_len, blocks // 2 * block_len)
-        pairs = ((k_hbm, k_ref), (q_hbm, q_ref), (g_hbm, g_ref))
+        pairs = ((k_hbm, k_ref), (q_hbm, q_ref))
         copies.append(
             [
                 pltpu.make_async_copy(there.at[at], here.at[at], sems.at[half, i])
                 for i, (there, here) in enumerate(pairs)
             ]
         )
+    copies[1].append(pltpu.make_async_copy(g_hbm, g_ref, sems.at[0, 2]))
     copies[0] += [
         pltpu.make_async_copy(delta_hbm, delta_ref, small_sems.at[0]),
         pltpu.make_async_copy(partner_hbm, partner_ref, small_sems.at[1]),
@@ -189,12 +192,13 @@
     for copy in copies[0] + copies[1]:
         copy.start()
 
+    tails, sent = [], []
     for j in range(blocks):
         if j % (blocks // 2) == 0:
             for copy in copies[j // (blocks // 2)]:
                 copy.wait()
         at = slice(j * block_len, (j + 1) * block_len)
-        qb, kb, gb = q_ref[at, :], k_ref[at, :], g_ref[at, :]
+        qb, kb = q_ref[at, :], k_ref[at, :]
         scores = dot(kb, head_stack(qb, score_scale), ((1,), (1,)))
         top = jnp.max(scores, axis=0, keepdims=True)
         lse = top + jnp.log(jnp.sum(jnp.exp(scores - top), axis=0, keepdims=True))
@@ -218,10 +222,35 @@
         )
         to = slice(j * pieces, (j + 1) * pieces)
         rows_ref[to, 0:512] = fold(qb, pieces)
-        rows_ref[to, 512:1024] = fold(gb, pieces)
+        for other in range(j + 1 if j == blocks // 2 else 0):
+            gb = g_ref[other * block_len : (other + 1) * block_len, :]
+            rows_ref[other * pieces : (other + 1) * pieces, 512:1024] = fold(gb, pieces)
+        if j > blocks // 2:
+            rows_ref[to, 512:1024] = fold(g_ref[at, :], pieces)
         rows_ref[to, 1024:1152] = jnp.concatenate([left, deltas, tags], axis=1).astype(BF16)
 
-    send_rows(out_ref, rows_ref, 1024, None)
+        if j == blocks // 2:
+            tails.append(send_half(out_ref, rows_ref, 1024, 0))
+            sent.append(
+                pltpu.make_async_copy(
+                    out_ref.at[:, :, pl.ds(0, 1024)],
+                    out_hbm.at[:, :, pl.ds(0, 1024)],
+                    out_sems.at[0],
+                )
+            )
+            sent[0].start()
+    tails.append(send_half(out_ref, rows_ref, 1024, 1))
+    store_stats(out_ref, 2048, *tails)
+    sent.append(
+        pltpu.make_async_copy(
+            out_ref.at[:, :, pl.ds(1024, 1152)],
+            out_hbm.at[:, :, pl.ds(1024, 1152)],
+            out_sems.at[1],
+        )
+    )
+    sent[1].start()
+    for copy in sent:
+        copy.wait()
 
 
 def partner_pick(place):
@@ -499,6 +528,7 @@
         [wide_slots, ((blocks, LANES), F32)],
         [partner, queries, keys, dout, delta],
         scratch=[
+            pltpu.VMEM(wide_slots[0], BF16),
             pltpu.VMEM((rows, 1152), BF16),
             pltpu.SMEM((blocks,), jnp.int32),
             buffer,
@@ -507,8 +537,10 @@
             pltpu.VMEM(delta.shape, F32),
             pltpu.SemaphoreType.DMA((2, 3)),
             pltpu.SemaphoreType.DMA((2,)),
+            pltpu.SemaphoreType.DMA((2,)),
         ],
         in_hbm=True,
+        out_hbm=1,
         limit=WHOLE_LIMIT,
     )
     spread = exchange(sent)

time: 147 us -> 148 us (level)
  no operation moved by 1% of the time
where the time goes in v6:
time: 148 us
  blocking collectives  129 us (87%)
  Pallas kernels  17.9 us (12%)
    all_to_all x4, blocking collectives, exchange(): return lax.all_to_all(x, 'seq', split_axis=0, concat_axis=0, tiled=True)  129 us
    pallas_call x5, Pallas kernels, call(): pl.pallas_call(kernel, out_shape=shapes, in_specs=[whole(pl.ANY if in_hbm...  17.9 us

profile of v6, /device:TPU:1, one launch (start us, length us, event | category | flops | bytes accessed | tf_op | source)
XLA Modules:
  0.0 147.6 jit_solution(7507139993070336977)
XLA Ops:
  0.6 4.8 %shard_map.102 = (bf16[64,4,2176]{2,1,0:T(4,128)(2,1)}, f32[8,128]{1,0:T(8,128)}) custom-call(s32[8]{0:T(128)} %partner_hbm.1, bf16[2048,128]{1,0:T(8,128)(2,1)} %q_ref.1, bf16[2048,128]{1,0:T(8,128)(2,1)} %k_ref.3, bf16[2048,128]{1,0:T(8,128)(2,1)} %g_ref.1, f32[2,2048]{1,0:T(2,128)} %delta_ref.1), custom_call_target="tpu_custom_call" | custom-call | flops 268435456 | bytes 2707488 | tf_op jit(solution)/shard_map/pallas_call | solution.py:505
  5.5 43.1 %all_to_all.20.in_ref = bf16[64,4,2176]{2,1,0:T(4,128)(2,1)S(1)} all-to-all(bf16[64,4,2176]{2,1,0:T(4,128)(2,1)} %get-tuple-element.16), channel_id=1, replica_groups=mesh['seq'=64,'head'=4] {'seq'}, dimensions={0} | all-to-all | bytes 2228224 | tf_op jit(solution)/shard_map/all_to_all | solution.py:517
  48.6 1.1 shard_map.103
  49.7 0.0 copy-start
  49.7 0.0 copy-start.1
  49.7 0.0 copy-start.4
  49.7 0.0 copy-start.6
  49.7 36.1 %all_to_all.21.in_ref = bf16[64,4,2176]{2,1,0:T(4,128)(2,1)S(1)} all-to-all(bf16[64,4,2176]{2,1,0:T(4,128)(2,1)S(1)} %get-tuple-element.18), channel_id=1, replica_groups=mesh['seq'=64,'head'=4] {'seq'}, dimensions={0} | all-to-all | bytes 2228224 | tf_op jit(solution)/shard_map/all_to_all | solution.py:517
  85.8 0.0 copy-done
  85.8 0.0 copy-done.1
  85.8 0.0 copy-done.4
  85.8 0.0 copy-done.6
  85.8 5.9 %shard_map.104 = (bf16[64,4,1152]{2,1,0:T(4,128)(2,1)S(1)}, bf16[2048,128]{1,0:T(8,128)(2,1)S(1)}, bf16[2048,128]{1,0:T(8,128)(2,1)S(1)}, f32[8,128]{1,0:T(8,128)S(1)}) custom-call(bf16[64,4,2176]{2,1,0:T(4,128)(2,1)S(1)} %all_to_all.21.in_ref, bf16[2048,128]{1,0:T(8,128)(2,1)S(1)} %copy-done, bf16[2048,128]{1,0:T(8,128)(2,1)S(1)} %copy-done.1, ...), custom_call_target="tpu_custom_call" | custom-call | flops 268435456 | bytes 3842048 | tf_op jit(solution)/shard_map/pallas_call | solution.py:505
  91.7 24.7 %all_to_all.22.in_ref = bf16[64,4,1152]{2,1,0:T(4,128)(2,1)S(1)} all-to-all(bf16[64,4,1152]{2,1,0:T(4,128)(2,1)S(1)} %get-tuple-element.20), channel_id=1, replica_groups=mesh['seq'=64,'head'=4] {'seq'}, dimensions={0} | all-to-all | bytes 1179648 | tf_op jit(solution)/shard_map/all_to_all | solution.py:517
  116.5 0.0 copy-start.2
  116.5 0.0 copy-start.3
  116.5 0.0 copy-start.5
  116.5 0.7 shard_map.105
  117.2 24.8 %all_to_all.23.in_ref = bf16[64,4,1152]{2,1,0:T(4,128)(2,1)S(1)} all-to-all(bf16[64,4,1152]{2,1,0:T(4,128)(2,1)S(1)} %shard_map.105), channel_id=1, replica_groups=mesh['seq'=64,'head'=4] {'seq'}, dimensions={0} | all-to-all | bytes 1179648 | tf_op jit(solution)/shard_map/all_to_all | solution.py:517
  141.9 0.0 copy-done.2
  141.9 0.0 copy-done.3
  142.0 0.0 copy-done.5
  142.0 5.5 %shard_map.106 = (bf16[2048,128]{1,0:T(8,128)(2,1)}, bf16[2048,128]{1,0:T(8,128)(2,1)}, bf16[2048,128]{1,0:T(8,128)(2,1)}, f32[128,64]{1,0:T(8,128)}) custom-call(bf16[64,4,1152]{2,1,0:T(4,128)(2,1)S(1)} %all_to_all.23.in_ref, bf16[2048,128]{1,0:T(8,128)(2,1)S(1)} %copy-done.2, bf16[2048,128]{1,0:T(8,128)(2,1)S(1)} %copy-done, ...), custom_call_target="tpu_custom_call" | custom-call | flops 268435456 | bytes 5394432 | tf_op jit(solution)/shard_map/pallas_call | solution.py:505
Async XLA Ops:
  49.7 36.1 %copy-start = (bf16[2048,128]{1,0:T(8,128)(2,1)S(1)}, bf16[2048,128]{1,0:T(8,128)(2,1)}, u32[]{:S(2)}) copy-start(bf16[2048,128]{1,0:T(8,128)(2,1)} %k_ref.3) | copy-start | bytes 1572868
  49.7 36.1 %copy-start.1 = (bf16[2048,128]{1,0:T(8,128)(2,1)S(1)}, bf16[2048,128]{1,0:T(8,128)(2,1)}, u32[]{:S(2)}) copy-start(bf16[2048,128]{1,0:T(8,128)(2,1)} %v_ref.3) | copy-start | bytes 1572868
  49.7 36.1 %copy-start.4 = (f32[2,64,64]{2,1,0:T(8,128)S(1)}, f32[2,64,64]{2,1,0:T(8,128)}, u32[]{:S(2)}) copy-start(f32[2,64,64]{2,1,0:T(8,128)} %w_ref.3) | copy-start | bytes 98308
  49.7 36.1 %copy-start.6 = (f32[8,128]{1,0:T(8,128)S(1)}, f32[8,128]{1,0:T(8,128)}, u32[]{:S(2)}) copy-start(f32[8,128]{1,0:T(8,128)} %get-tuple-element.19.summary_ref) | copy-start | bytes 12292
  116.5 25.5 %copy-start.2 = (bf16[2048,128]{1,0:T(8,128)(2,1)S(1)}, bf16[2048,128]{1,0:T(8,128)(2,1)}, u32[]{:S(2)}) copy-start(bf16[2048,128]{1,0:T(8,128)(2,1)} %q_ref.1) | copy-start | bytes 1572868
  116.5 25.5 %copy-start.3 = (bf16[2048,128]{1,0:T(8,128)(2,1)S(1)}, bf16[2048,128]{1,0:T(8,128)(2,1)}, u32[]{:S(2)}) copy-start(bf16[2048,128]{1,0:T(8,128)(2,1)} %g_ref.1) | copy-start | bytes 1572868
  116.5 25.5 %copy-start.5 = (f32[2,2048]{1,0:T(2,128)S(1)}, f32[2,2048]{1,0:T(2,128)}, u32[]{:S(2)}) copy-start(f32[2,2048]{1,0:T(2,128)} %delta_ref.1) | copy-start | bytes 49156
